TPU v7x, 512 devices: a whole 4x8x8 slice. The times are simulated.
512 devices in a mesh: tile: 64 (over z, y), win: 8 (over x, core).
Axes of the slice: x: 4, y: 8, z: 8, core: 2. Of those that a mesh axis runs over, the one named last changes fastest.
Arguments:
- spectra: bfloat16 [16, 512, 4096], P('win', 'tile'), may hold values from -6 to 6
- requests: int32 [64, 64, 2], P('tile'), may hold values from 0 to 7
- pair_first: int32 [16384], P('tile'), may hold values from 0 to 127
- pair_second: int32 [16384], P('tile'), may hold values from 0 to 127
- pair_count: int32 [64], P('tile'), may hold values from 1 to 256, 10240 in all
Outputs:
- correlations: float32 [16384, 1024], P(('tile', 'win'))
Inputs may be any that keep to these rules, and one draw needn't show every extreme that they name: `pair_count`: some tile has all 256 pairs live.
All inputs are finite; a program needn't handle non-finite values. No bound on the sum of `pair_count` on one device may be relied on, other than what follows from the above.
Results may differ from a plain program's by a relative error of at most 0.0029.
Values may be sent and summed in bfloat16 or wider, within the bound.
No kernel may reach another device: no remote copies, remote signals or barrier semaphores. Data moves between devices by JAX's collectives and lax.ppermute only.
A program may use at most 64 MiB of HBM per device.

v0:
```python
import math

import jax
import jax.numpy as jnp
import numpy as np
from jax import lax
from jax.experimental import pallas as pl
from jax.experimental.pallas import tpu as pltpu
from jax.sharding import PartitionSpec as P

LAGS = 1024
BINS = 2048
HALF = BINS // 2
LANES = 128
BLOCKS = HALF // LANES
ROWS = 4 * BLOCKS
VMEM_LIMIT = 48 * 1024 * 1024


def fold_table():
    lags = np.arange(LAGS, dtype=np.int64) - LAGS // 2
    turns = (np.arange(HALF, dtype=np.int64)[:, None] * lags[None, :]) % BINS
    angle = turns * (2.0 * math.pi / BINS)
    cosine, sine = np.cos(angle), -np.sin(angle)
    sign = 1.0 - 2.0 * (lags % 2)
    cosine[0] = (1.0 + sign) / 2
    sine[0] = (1.0 - sign) / 2
    return np.concatenate([cosine, sine]).astype(np.float32)


def whiten_kernel(wanted, spectra, send, blocks, white):
    hours, homes = spectra.shape[0], spectra.shape[1]
    values = spectra[...].reshape(hours * homes, 2 * BINS).astype(jnp.float32)
    real_part, imag_part = values[:, :BINS], values[:, BINS:]
    power = real_part * real_part + imag_part * imag_part
    level = jnp.mean(power, axis=-1, keepdims=True)
    factor = lax.rsqrt(power + 0.1 * level + 1e-06)
    row = lax.broadcasted_iota(jnp.int32, (2 * LANES, LANES), 0)
    column = lax.broadcasted_iota(jnp.int32, (2 * LANES, LANES), 1)
    mirror = jnp.where(row == LANES - column, 1.0, 0.0).astype(jnp.bfloat16)
    for part, base in ((real_part * factor, 0), (imag_part * factor, 2 * BLOCKS)):
        rounded = part.astype(jnp.bfloat16)
        for j in range(BLOCKS):
            blocks[:, base + j, :] = rounded[:, j * LANES : (j + 1) * LANES].astype(jnp.float32)
            near = 2 * BLOCKS - 1 - j
            head = near + 1 if j else BLOCKS
            pair = jnp.concatenate(
                [rounded[:, near * LANES : (near + 1) * LANES], rounded[:, head * LANES : (head + 1) * LANES]], axis=1
            )
            blocks[:, base + BLOCKS + j, :] = jnp.dot(pair, mirror, preferred_element_type=jnp.float32)
    white[...] = blocks[...].reshape(white.shape).astype(jnp.bfloat16)
    tiles, cap = send.shape[0], send.shape[1]

    @pl.loop(0, tiles, unroll=4)
    def _(tile):
        for c in range(cap):
            station = wanted[tile, c]
            for hour in range(hours):
                send[tile, c, hour] = white[hour, station]


def stack_kernel(first, second, count, slots, table, series, weights, sums, folded, sem):
    pairs, hours = sums.shape[0], slots.shape[1]
    load = pltpu.make_async_copy(table, weights, sem)
    load.start()
    place = lax.broadcasted_iota(jnp.int32, (BLOCKS, LANES), 0) + lax.broadcasted_iota(jnp.int32, (BLOCKS, LANES), 1)
    corner = place == 0

    @pl.loop(0, pairs, unroll=8)
    def _(p):
        a, b = first[p], second[p]
        total_real, total_imag = 0.0, 0.0
        for hour in range(hours):
            left = slots[a, hour].astype(jnp.float32)
            right = slots[b, hour].astype(jnp.float32)
            left_real, left_imag = left[: 2 * BLOCKS], left[2 * BLOCKS :]
            right_real, right_imag = right[: 2 * BLOCKS], right[2 * BLOCKS :]
            total_real = total_real + (left_real * right_real + left_imag * right_imag)
            total_imag = total_imag + (left_imag * right_real - left_real * right_imag)
        low, high = total_real[:BLOCKS], total_real[BLOCKS:]
        sums[p, :BLOCKS] = low + high
        sums[p, BLOCKS:] = jnp.where(corner, low - high, total_imag[:BLOCKS] - total_imag[BLOCKS:])

    live = lax.broadcasted_iota(jnp.int32, (pairs, LANES), 0) < count[0]
    for j in range(2 * BLOCKS):
        folded[:, j * LANES : (j + 1) * LANES] = jnp.where(live, sums[:, j, :], 0.0).astype(jnp.bfloat16)
    load.wait()
    for j in range(0, LAGS, 256):
        series[:, j : j + 256] = jnp.dot(
            folded[...], weights[:, j : j + 256], preferred_element_type=jnp.float32
        ).astype(jnp.bfloat16)


def body(spectra, requests, pair_first, pair_second, pair_count, table):
    hours, homes = spectra.shape[0], spectra.shape[1]
    tiles, cap = requests.shape[1], requests.shape[2]
    pairs = pair_first.shape[0]
    windows = lax.axis_size("win")
    wanted = lax.all_to_all(requests[0], "tile", 0, 0, tiled=True)
    vmem = pl.BlockSpec(memory_space=pltpu.VMEM)
    smem = pl.BlockSpec(memory_space=pltpu.SMEM)
    send = pl.pallas_call(
        whiten_kernel,
        out_shape=jax.ShapeDtypeStruct((tiles, cap, hours, ROWS, LANES), jnp.bfloat16),
        in_specs=[smem, vmem],
        out_specs=vmem,
        scratch_shapes=[
            pltpu.VMEM((hours * homes, ROWS, LANES), jnp.float32),
            pltpu.VMEM((hours, homes, ROWS, LANES), jnp.bfloat16),
        ],
        compiler_params=pltpu.CompilerParams(vmem_limit_bytes=VMEM_LIMIT),
    )(wanted, spectra)
    slots = lax.all_to_all(send, "tile", 0, 0, tiled=True).reshape(tiles * cap, hours, ROWS, LANES)
    series = pl.pallas_call(
        stack_kernel,
        out_shape=jax.ShapeDtypeStruct((pairs, LAGS), jnp.bfloat16),
        in_specs=[smem, smem, smem, vmem, pl.BlockSpec(memory_space=pl.ANY)],
        out_specs=vmem,
        scratch_shapes=[
            pltpu.VMEM((BINS, LAGS), jnp.bfloat16),
            pltpu.VMEM((pairs, 2 * BLOCKS, LANES), jnp.float32),
            pltpu.VMEM((pairs, BINS), jnp.bfloat16),
            pltpu.SemaphoreType.DMA,
        ],
        compiler_params=pltpu.CompilerParams(vmem_limit_bytes=VMEM_LIMIT),
    )(pair_first, pair_second, pair_count, slots, table)
    parts = lax.all_to_all(series.reshape(windows, pairs // windows, LAGS), "win", 0, 0, tiled=True)
    scale = 1.0 / math.sqrt(BINS * hours * windows)
    return jnp.sum(parts.astype(jnp.float32), axis=0) * scale


def solution(mesh):
    table = fold_table().astype(jnp.bfloat16)
    mapped = jax.shard_map(
        body,
        mesh=mesh,
        in_specs=(P("win", "tile", None), P("tile", None, None), P("tile"), P("tile"), P("tile"), P()),
        out_specs=P(("tile", "win"), None),
        check_vma=False,
    )

    def run(spectra, requests, pair_first, pair_second, pair_count):
        return mapped(spectra, requests, pair_first, pair_second, pair_count, jnp.asarray(table))

    return run
```

profile of v0, /device:TPU:1, one launch (start us, length us, event | category | flops | bytes accessed | tf_op | source)
XLA Modules:
  0.0 110.5 jit_solution(15187436741169953136)
XLA Ops:
  0.0 0.8 copy.8
  0.8 27.8 %all_to_all.21 = s32[64,1,2]{2,1,0:T(1,128)S(1)} all-to-all(s32[64,1,2]{2,1,0:T(1,128)S(1)} %copy.8), channel_id=1, replica_groups=mesh['tile'=64,'win'=8] {'tile'}, dimensions={0} | all-to-all | bytes 1024 | tf_op jit(solution)/shard_map/all_to_all | solution.py:99
  28.5 0.0 copy-start.1
  28.5 0.9 copy-done.1
  29.4 1.7 %shard_map.64 = bf16[64,2,2,32,128]{4,3,2,1,0:T(8,128)(2,1)S(1)} custom-call(s32[64,2]{1,0:T(8,128)S(1)} %bitcast.6, bf16[2,8,4096]{2,1,0:T(8,128)(2,1)S(1)} %copy-done.1), custom_call_target="tpu_custom_call" | custom-call | tf_op jit(solution)/shard_map/pallas_call | solution.py:102
  31.1 0.0 copy-start
  31.1 1.3 %copy-done = bf16[64,2,2,32,128]{4,3,2,1,0:T(8,128)(2,1)} copy-done((bf16[64,2,2,32,128]{4,3,2,1,0:T(8,128)(2,1)}, bf16[64,2,2,32,128]{4,3,2,1,0:T(8,128)(2,1)S(1)}, u32[]{:S(2)}) %copy-start) | copy-done | bytes 2097176
  32.5 0.0 copy-start.2
  32.5 0.0 copy-start.3
  32.5 4.8 %all-to-all-start.1 = ((bf16[64,2,2,32,128]{4,3,2,1,0:T(8,128)(2,1)}), bf16[64,2,2,32,128]{4,3,2,1,0:T(8,128)(2,1)S(1)}, u32[]{:S(2)}, u32[]{:S(2)}) async-start(bf16[64,2,2,32,128]{4,3,2,1,0:T(8,128)(2,1)} %copy-done), calls=%async_computation.1 | async-start | bytes 4194304 | tf_op jit(solution)/shard_map/all_to_all | solution.py:113
  38.0 47.7 %all-to-all-done.1 = bf16[64,2,2,32,128]{4,3,2,1,0:T(8,128)(2,1)S(1)} async-done(((bf16[64,2,2,32,128]{4,3,2,1,0:T(8,128)(2,1)}), bf16[64,2,2,32,128]{4,3,2,1,0:T(8,128)(2,1)S(1)}, u32[]{:S(2)}, u32[]{:S(2)}) %all-to-all-start.1) | async-done | bytes 2097184 | tf_op jit(solution)/shard_map/all_to_all | solution.py:113
  85.6 0.0 copy-done.2
  85.6 0.0 copy-done.3
  85.6 5.3 %shard_map.65 = bf16[256,1024]{1,0:T(8,128)(2,1)S(1)} custom-call(s32[256]{0:T(256)S(1)} %copy-done.2, s32[256]{0:T(256)S(1)} %copy-done.3, s32[1]{0:T(128)S(6)} %copy.12.count, bf16[128,2,32,128]{3,2,1,0:T(8,128)(2,1)S(1)} %bitcast.4, bf16[2048,1024]{1,0:T(8,128)(2,1)} %constant.6.clone.table), custom_call_target="tpu_custom_call" | custom-call | tf_op jit(solution)/shard_map/pallas_call | solution.py:114
  90.9 18.8 %all_to_all.22 = bf16[8,32,1024]{2,1,0:T(8,128)(2,1)S(1)} all-to-all(bf16[8,32,1024]{2,1,0:T(8,128)(2,1)S(1)} %bitcast.5), channel_id=1, replica_groups=mesh['tile'=64,'win'=8] {'win'}, dimensions={0} | all-to-all | bytes 1048576 | tf_op jit(solution)/shard_map/all_to_all | solution.py:127
  109.7 0.1 convert_reduce_fusion
  109.8 0.7 broadcast_multiply_fusion
Async XLA Ops:
  28.5 0.9 copy-start.1
  31.1 1.3 %copy-start = (bf16[64,2,2,32,128]{4,3,2,1,0:T(8,128)(2,1)}, bf16[64,2,2,32,128]{4,3,2,1,0:T(8,128)(2,1)S(1)}, u32[]{:S(2)}) copy-start(bf16[64,2,2,32,128]{4,3,2,1,0:T(8,128)(2,1)S(1)} %shard_map.64) | copy-start | bytes 6291460
  32.5 53.1 %copy-start.2 = (s32[256]{0:T(256)S(1)}, s32[256]{0:T(256)}, u32[]{:S(2)}) copy-start(s32[256]{0:T(256)} %first.1) | copy-start | bytes 3076
  32.5 53.1 %copy-start.3 = (s32[256]{0:T(256)S(1)}, s32[256]{0:T(256)}, u32[]{:S(2)}) copy-start(s32[256]{0:T(256)} %second.1) | copy-start | bytes 3076
  32.5 53.1 %all-to-all-start.1 = ((bf16[64,2,2,32,128]{4,3,2,1,0:T(8,128)(2,1)}), bf16[64,2,2,32,128]{4,3,2,1,0:T(8,128)(2,1)S(1)}, u32[]{:S(2)}, u32[]{:S(2)}) async-start(bf16[64,2,2,32,128]{4,3,2,1,0:T(8,128)(2,1)} %copy-done), calls=%async_computation.1 | async-start | bytes 4194304 | tf_op jit(solution)/shard_map/all_to_all | solution.py:113
where the time goes:
time: 111 us; the launch traced here: 110 us
  waiting for transfers between devices  47.7 us (43%)
  blocking collectives  46.6 us (42%)
  Pallas kernels  6.95 us (6%)
  starting transfers between devices  4.82 us (4%)
  local copies, waits for them, and re-layouts  3 us (3%)
    all_to_all x1, waiting for transfers between devices, body(): lax.all_to_all(send, 'tile', 0, 0, tiled=True)  47.7 us
    all_to_all x1, blocking collectives, body(): wanted = lax.all_to_all(requests[0], 'tile', 0, 0, tiled=True)  27.8 us
    all_to_all x1, blocking collectives, body(): lax.all_to_all(series.reshape(windows, pairs // windows, LAGS), 'win', 0,...  18.8 us
    pallas_call x1, Pallas kernels, body(): pl.pallas_call(stack_kernel, out_shape=jax.ShapeDtypeStruct((pairs, LAGS)...  5.26 us
    all_to_all x1, starting transfers between devices, body(): lax.all_to_all(send, 'tile', 0, 0, tiled=True)  4.82 us
    unnamed x8, local copies, waits for them, and re-layouts  2.24 us
  transfers between devices with their start and end apart: 1, of which 1 were waited for; matrix products, arithmetic and copies ran while one was open for 0% of the time, Pallas kernels for 0%

commit v1 on v0

--- a/solution.py
+++ b/solution.py
@@ -6,6 +6,7 @@
 from jax import lax
 from jax.experimental import pallas as pl
 from jax.experimental.pallas import tpu as pltpu
+from jax.sharding import Mesh
 from jax.sharding import PartitionSpec as P
 
 LAGS = 1024
@@ -14,6 +15,7 @@
 LANES = 128
 BLOCKS = HALF // LANES
 ROWS = 4 * BLOCKS
+AXES = ("z", "y", "x", "core")
 VMEM_LIMIT = 48 * 1024 * 1024
 
 
@@ -28,7 +30,7 @@
     return np.concatenate([cosine, sine]).astype(np.float32)
 
 
-def whiten_kernel(wanted, spectra, send, blocks, white):
+def whiten_kernel(spectra, send, blocks):
     hours, homes = spectra.shape[0], spectra.shape[1]
     values = spectra[...].reshape(hours * homes, 2 * BINS).astype(jnp.float32)
     real_part, imag_part = values[:, :BINS], values[:, BINS:]
@@ -48,21 +50,28 @@
                 [rounded[:, near * LANES : (near + 1) * LANES], rounded[:, head * LANES : (head + 1) * LANES]], axis=1
             )
             blocks[:, base + BLOCKS + j, :] = jnp.dot(pair, mirror, preferred_element_type=jnp.float32)
-    white[...] = blocks[...].reshape(white.shape).astype(jnp.bfloat16)
-    tiles, cap = send.shape[0], send.shape[1]
-
-    @pl.loop(0, tiles, unroll=4)
-    def _(tile):
-        for c in range(cap):
-            station = wanted[tile, c]
-            for hour in range(hours):
-                send[tile, c, hour] = white[hour, station]
+    for item in range(hours * homes):
+        white = blocks[item].astype(jnp.bfloat16)
+        for peer in range(send.shape[0]):
+            send[peer, item] = white
 
 
-def stack_kernel(first, second, count, slots, table, series, weights, sums, folded, sem):
+def pick_kernel(wanted, place, held, send):
+    peers, sources, cap, hours = send.shape[:4]
+    homes = held.shape[1] // hours
+    base, source_step = place[0], place[1]
+
+    @pl.loop(0, peers)
+    def _(peer):
+        for source in range(sources):
+            for c in range(cap):
+                station = wanted[peer, base + source * source_step + c]
+                for hour in range(hours):
+                    send[peer, source, c, hour] = held[source, hour * homes + station]
+
+
+def stack_kernel(first, second, count, slots, weights, series, sums, folded):
     pairs, hours = sums.shape[0], slots.shape[1]
-    load = pltpu.make_async_copy(table, weights, sem)
-    load.start()
     place = lax.broadcasted_iota(jnp.int32, (BLOCKS, LANES), 0) + lax.broadcasted_iota(jnp.int32, (BLOCKS, LANES), 1)
     corner = place == 0
 
@@ -84,58 +93,97 @@
     live = lax.broadcasted_iota(jnp.int32, (pairs, LANES), 0) < count[0]
     for j in range(2 * BLOCKS):
         folded[:, j * LANES : (j + 1) * LANES] = jnp.where(live, sums[:, j, :], 0.0).astype(jnp.bfloat16)
-    load.wait()
     for j in range(0, LAGS, 256):
         series[:, j : j + 256] = jnp.dot(
             folded[...], weights[:, j : j + 256], preferred_element_type=jnp.float32
         ).astype(jnp.bfloat16)
 
 
+def grid_groups(depth, height, width, cores):
+    def number(z, y, x, core):
+        return ((z * height + y) * width + x) * cores + core
+
+    def along_z(core):
+        return [[number(z, y, x, core) for z in range(depth)] for y in range(height) for x in range(width)]
+
+    def along_y(core):
+        return [[number(z, y, x, core) for y in range(height)] for z in range(depth) for x in range(width)]
+
+    return along_z(0) + along_y(1), along_y(0) + along_z(1)
+
+
 def body(spectra, requests, pair_first, pair_second, pair_count, table):
     hours, homes = spectra.shape[0], spectra.shape[1]
     tiles, cap = requests.shape[1], requests.shape[2]
     pairs = pair_first.shape[0]
-    windows = lax.axis_size("win")
-    wanted = lax.all_to_all(requests[0], "tile", 0, 0, tiled=True)
+    depth, height, width, cores = (lax.axis_size(name) for name in AXES)
+    side = depth
+    windows = width * cores
+    core = lax.axis_index("core")
+    z, y = lax.axis_index("z"), lax.axis_index("y")
+    stage_one, stage_two = grid_groups(depth, height, width, cores)
     vmem = pl.BlockSpec(memory_space=pltpu.VMEM)
     smem = pl.BlockSpec(memory_space=pltpu.SMEM)
+    params = pltpu.CompilerParams(vmem_limit_bytes=VMEM_LIMIT)
+
+    wanted = lax.all_gather(
+        requests.reshape(1, tiles * cap), AXES, axis=0, axis_index_groups=stage_two, tiled=True
+    )
+    copies = pl.pallas_call(
+        whiten_kernel,
+        out_shape=jax.ShapeDtypeStruct((side, hours * homes, ROWS, LANES), jnp.bfloat16),
+        in_specs=[vmem],
+        out_specs=vmem,
+        scratch_shapes=[pltpu.VMEM((hours * homes, ROWS, LANES), jnp.float32)],
+        compiler_params=params,
+    )(spectra)
+    held = lax.all_to_all(copies, AXES, 0, 0, axis_index_groups=stage_one, tiled=True)
+    first_core = core == 0
+    place = jnp.stack(
+        [
+            jnp.where(first_core, y * cap, z * height * cap),
+            jnp.where(first_core, height * cap, cap),
+        ]
+    )
     send = pl.pallas_call(
-        whiten_kernel,
-        out_shape=jax.ShapeDtypeStruct((tiles, cap, hours, ROWS, LANES), jnp.bfloat16),
-        in_specs=[smem, vmem],
+        pick_kernel,
+        out_shape=jax.ShapeDtypeStruct((side, side, cap, hours, ROWS, LANES), jnp.bfloat16),
+        in_specs=[smem, smem, vmem],
         out_specs=vmem,
-        scratch_shapes=[
-            pltpu.VMEM((hours * homes, ROWS, LANES), jnp.float32),
-            pltpu.VMEM((hours, homes, ROWS, LANES), jnp.bfloat16),
-        ],
-        compiler_params=pltpu.CompilerParams(vmem_limit_bytes=VMEM_LIMIT),
-    )(wanted, spectra)
-    slots = lax.all_to_all(send, "tile", 0, 0, tiled=True).reshape(tiles * cap, hours, ROWS, LANES)
+        compiler_params=params,
+    )(wanted, place, held)
+    slots = lax.all_to_all(send, AXES, 0, 0, axis_index_groups=stage_two, tiled=True)
+
+    def where_held(slot):
+        home, c = slot // cap, slot % cap
+        turned = ((home % height) * depth + home // height) * cap + c
+        return jnp.where(first_core, turned, slot)
+
     series = pl.pallas_call(
         stack_kernel,
         out_shape=jax.ShapeDtypeStruct((pairs, LAGS), jnp.bfloat16),
-        in_specs=[smem, smem, smem, vmem, pl.BlockSpec(memory_space=pl.ANY)],
+        in_specs=[smem, smem, smem, vmem, vmem],
         out_specs=vmem,
         scratch_shapes=[
-            pltpu.VMEM((BINS, LAGS), jnp.bfloat16),
             pltpu.VMEM((pairs, 2 * BLOCKS, LANES), jnp.float32),
             pltpu.VMEM((pairs, BINS), jnp.bfloat16),
-            pltpu.SemaphoreType.DMA,
         ],
-        compiler_params=pltpu.CompilerParams(vmem_limit_bytes=VMEM_LIMIT),
-    )(pair_first, pair_second, pair_count, slots, table)
-    parts = lax.all_to_all(series.reshape(windows, pairs // windows, LAGS), "win", 0, 0, tiled=True)
+        compiler_params=params,
+    )(where_held(pair_first), where_held(pair_second), pair_count, slots.reshape(tiles * cap, hours, ROWS, LANES), table)
+    parts = lax.all_to_all(series.reshape(windows, pairs // windows, LAGS), ("x", "core"), 0, 0, tiled=True)
     scale = 1.0 / math.sqrt(BINS * hours * windows)
     return jnp.sum(parts.astype(jnp.float32), axis=0) * scale
 
 
 def solution(mesh):
     table = fold_table().astype(jnp.bfloat16)
+    devices = mesh.devices
+    grid = Mesh(devices.reshape(8, 8, 4, 2), AXES)
     mapped = jax.shard_map(
         body,
-        mesh=mesh,
-        in_specs=(P("win", "tile", None), P("tile", None, None), P("tile"), P("tile"), P("tile"), P()),
-        out_specs=P(("tile", "win"), None),
+        mesh=grid,
+        in_specs=(P(("x", "core"), ("z", "y"), None), P(("z", "y"), None, None), P(("z", "y")), P(("z", "y")), P(("z", "y")), P()),
+        out_specs=P(AXES, None),
         check_vma=False,
     )
 

time: 111 us -> 94 us (0.85)
  waiting for transfers between devices: 47.7 us -> 28.7 us
  starting transfers between devices: 4.82 us -> 13.7 us
  blocking collectives: 46.6 us -> 38.3 us
  Pallas kernels: 6.95 us -> 8.93 us
    all_to_all x2 -> x1, blocking collectives: 46.6 us -> 16.7 us  [body(): lax.all_to_all(series.reshape(windows, pairs // windows, LAGS), ('x', 'co...]
    all_gather x0 -> x1, blocking collectives: none -> 21.6 us  [body(): lax.all_gather(requests.reshape(1, tiles * cap), AXES, axis=0, axis_index...]
    all_to_all x1 -> x2, waiting for transfers between devices: 47.7 us -> 28.7 us  [the longest x1 28.7 us: body(): lax.all_to_all(send, AXES, 0, 0, axis_index_groups=stage_two, tiled=True)]
    all_to_all x1 -> x2, starting transfers between devices: 4.82 us -> 13.7 us  [the longest x1 7.65 us: body(): lax.all_to_all(copies, AXES, 0, 0, axis_index_groups=stage_one, tiled=True)]
    pallas_call x1, Pallas kernels: 5.26 us -> 6.53 us  [body(): pl.pallas_call(stack_kernel, out_shape=jax.ShapeDtypeStruct((pairs, LAGS)...]
    pallas_call x1 -> x2, Pallas kernels: 1.69 us -> 2.4 us  [the longest x1 1.43 us: body(): pl.pallas_call(whiten_kernel, out_shape=jax.ShapeDtypeStruct((side, hours...]
    unnamed x8 -> x12, local copies, waits for them, and re-layouts: 2.24 us -> 2.49 us
  transfers between devices with their start and end apart: 1 -> 2, of which waited for: 1 -> 1; matrix products, arithmetic and copies ran while one was open for 0% -> 0% of each run, Pallas kernels for 0% -> 0%
where the time goes in v1:
time: 94 us; the launch traced here: 93.7 us
  blocking collectives  38.3 us (41%)
  waiting for transfers between devices  28.7 us (31%)
  starting transfers between devices  13.7 us (15%)
  Pallas kernels  8.93 us (10%)
  local copies, waits for them, and re-layouts  2.49 us (3%)
    all_to_all x1, waiting for transfers between devices, body(): lax.all_to_all(send, AXES, 0, 0, axis_index_groups=stage_two, tiled=True)  28.7 us
    all_gather x1, blocking collectives, body(): lax.all_gather(requests.reshape(1, tiles * cap), AXES, axis=0, axis_index...  21.6 us
    all_to_all x1, blocking collectives, body(): lax.all_to_all(series.reshape(windows, pairs // windows, LAGS), ('x', 'co...  16.7 us
    all_to_all x1, starting transfers between devices, body(): lax.all_to_all(copies, AXES, 0, 0, axis_index_groups=stage_one, tiled=True)  7.65 us
    pallas_call x1, Pallas kernels, body(): pl.pallas_call(stack_kernel, out_shape=jax.ShapeDtypeStruct((pairs, LAGS)...  6.53 us
    all_to_all x1, starting transfers between devices, body(): lax.all_to_all(send, AXES, 0, 0, axis_index_groups=stage_two, tiled=True)  6.09 us
    unnamed x12, local copies, waits for them, and re-layouts  2.49 us
  transfers between devices with their start and end apart: 2, of which 1 were waited for; matrix products, arithmetic and copies ran while one was open for 0% of the time, Pallas kernels for 0%

profile of v1, /device:TPU:1, one launch (start us, length us, event | category | flops | bytes accessed | tf_op | source)
XLA Modules:
  0.0 93.7 jit_solution(8770628434286710574)
XLA Ops:
  0.0 0.0 copy-start.1
  0.0 0.9 copy-done.1
  0.9 0.0 copy-start.2
  0.9 1.4 %shard_map.64 = bf16[8,16,32,128]{3,2,1,0:T(8,128)(2,1)} custom-call(bf16[2,8,4096]{2,1,0:T(8,128)(2,1)S(1)} %copy-done.1), custom_call_target="tpu_custom_call" | custom-call | tf_op jit(solution)/shard_map/pallas_call | solution.py:132
  2.3 7.7 %all-to-all-start = ((bf16[8,16,32,128]{3,2,1,0:T(8,128)(2,1)}), bf16[8,16,32,128]{3,2,1,0:T(8,128)(2,1)S(1)}, u32[]{:S(2)}, u32[]{:S(2)}) async-start(bf16[8,16,32,128]{3,2,1,0:T(8,128)(2,1)} %shard_map.64), calls=%async_computation | async-start | bytes 2097152 | tf_op jit(solution)/shard_map/all_to_all | solution.py:140
  10.0 0.0 copy-done.2
  10.0 0.1 copy.11
  10.1 0.1 reshape.12
  10.2 21.6 %all-gather = s32[8,1,128]{2,1,0:T(1,128)S(1)} all-gather(s32[1,1,128]{2,1,0:T(1,128)S(1)} %reshape.12), channel_id=1, replica_groups={{0,8,16,24,32,40,48,56},{2,10,18,26,34,42,50,58},{4,12,20,28,36,44,52,6..., dimensions={0}, use_global_device_ids=true | all-gather | bytes 4608 | tf_op jit(solution)/shard_map/all_gather | solution.py:129
  31.8 0.1 pad_add_fusion.place
  31.9 0.0 all-to-all-done.held
  31.9 1.0 %shard_map.65 = bf16[8,8,2,2,32,128]{5,4,3,2,1,0:T(8,128)(2,1)S(1)} custom-call(s32[8,128]{1,0:T(8,128)S(1)} %bitcast.7, s32[2]{0:T(128)S(1)} %pad_add_fusion.place, bf16[8,16,32,128]{3,2,1,0:T(8,128)(2,1)S(1)} %all-to-all-done.held), custom_call_target="tpu_custom_call" | custom-call | tf_op jit(solution)/shard_map/pallas_call | solution.py:148
  32.9 0.0 copy-start
  32.9 1.3 %copy-done = bf16[8,8,2,2,32,128]{5,4,3,2,1,0:T(8,128)(2,1)} copy-done((bf16[8,8,2,2,32,128]{5,4,3,2,1,0:T(8,128)(2,1)}, bf16[8,8,2,2,32,128]{5,4,3,2,1,0:T(8,128)(2,1)S(1)}, u32[]{:S(2)}) %copy-start) | copy-done | bytes 2097176
  34.2 0.0 copy-start.3
  34.2 0.0 copy-start.4
  34.2 6.1 %all-to-all-start.1 = ((bf16[8,8,2,2,32,128]{5,4,3,2,1,0:T(8,128)(2,1)}), bf16[8,8,2,2,32,128]{5,4,3,2,1,0:T(8,128)(2,1)S(1)}, u32[]{:S(2)}, u32[]{:S(2)}) async-start(bf16[8,8,2,2,32,128]{5,4,3,2,1,0:T(8,128)(2,1)} %copy-done), calls=%async_computation.1 | async-start | bytes 4194304 | tf_op jit(solution)/shard_map/all_to_all | solution.py:155
  41.0 0.0 copy-done.3
  41.0 0.0 copy-done.4
  41.0 28.7 %all-to-all-done.1 = bf16[8,8,2,2,32,128]{5,4,3,2,1,0:T(8,128)(2,1)S(1)} async-done(((bf16[8,8,2,2,32,128]{5,4,3,2,1,0:T(8,128)(2,1)}), bf16[8,8,2,2,32,128]{5,4,3,2,1,0:T(8,128)(2,1)S(1)}, u32[]{:S(2)}, u32[]{:S(2)}) %all-to-all-start.1) | async-done | bytes 2097184 | tf_op jit(solution)/shard_map/all_to_all | solution.py:155
  69.7 6.5 %shard_map.66 = bf16[256,1024]{1,0:T(8,128)(2,1)S(1)} custom-call(s32[256]{0:T(256)S(1)} %get-tuple-element.5.first, s32[256]{0:T(256)S(1)} %get-tuple-element.6.second, s32[1]{0:T(128)S(6)} %copy.12.count, bf16[128,2,32,128]{3,2,1,0:T(8,128)(2,1)S(1)} %bitcast.5, bf16[2048,1024]{1,0:T(8,128)(2,1)} %constant.95.clone.weights), custom_call_target="tpu_custom_call" | custom-call | tf_op jit(solution)/shard_map/pallas_call | solution.py:162
  76.2 16.7 %all_to_all.15 = bf16[8,32,1024]{2,1,0:T(8,128)(2,1)S(1)} all-to-all(bf16[8,32,1024]{2,1,0:T(8,128)(2,1)S(1)} %bitcast.6), channel_id=1, replica_groups=mesh['z'=8,'y'=8,'x'=4,'core'=2] {'x','core'}, dimensions={0} | all-to-all | bytes 1048576 | tf_op jit(solution)/shard_map/all_to_all | solution.py:173
  93.0 0.1 convert_reduce_fusion
  93.1 0.7 broadcast_multiply_fusion
  (1 shorter events, 0.0 us)
Async XLA Ops:
  0.0 0.9 copy-start.1
  0.9 9.1 %copy-start.2 = (s32[1,64,2]{1,2,0:T(2,128)S(1)}, s32[1,64,2]{1,2,0:T(2,128)}, u32[]{:S(2)}) copy-start(s32[1,64,2]{1,2,0:T(2,128)} %param.7) | copy-start | bytes 1540
  2.3 29.6 %all-to-all-start = ((bf16[8,16,32,128]{3,2,1,0:T(8,128)(2,1)}), bf16[8,16,32,128]{3,2,1,0:T(8,128)(2,1)S(1)}, u32[]{:S(2)}, u32[]{:S(2)}) async-start(bf16[8,16,32,128]{3,2,1,0:T(8,128)(2,1)} %shard_map.64), calls=%async_computation | async-start | bytes 2097152 | tf_op jit(solution)/shard_map/all_to_all | solution.py:140
  32.9 1.3 %copy-start = (bf16[8,8,2,2,32,128]{5,4,3,2,1,0:T(8,128)(2,1)}, bf16[8,8,2,2,32,128]{5,4,3,2,1,0:T(8,128)(2,1)S(1)}, u32[]{:S(2)}) copy-start(bf16[8,8,2,2,32,128]{5,4,3,2,1,0:T(8,128)(2,1)S(1)} %shard_map.65) | copy-start | bytes 6291460
  34.2 6.8 %copy-start.3 = (s32[256]{0:T(256)S(1)}, s32[256]{0:T(256)}, u32[]{:S(2)}) copy-start(s32[256]{0:T(256)} %param.8) | copy-start | bytes 3076
  34.2 6.8 %copy-start.4 = (s32[256]{0:T(256)S(1)}, s32[256]{0:T(256)}, u32[]{:S(2)}) copy-start(s32[256]{0:T(256)} %param.9) | copy-start | bytes 3076
  34.2 35.5 %all-to-all-start.1 = ((bf16[8,8,2,2,32,128]{5,4,3,2,1,0:T(8,128)(2,1)}), bf16[8,8,2,2,32,128]{5,4,3,2,1,0:T(8,128)(2,1)S(1)}, u32[]{:S(2)}, u32[]{:S(2)}) async-start(bf16[8,8,2,2,32,128]{5,4,3,2,1,0:T(8,128)(2,1)} %copy-done), calls=%async_computation.1 | async-start | bytes 4194304 | tf_op jit(solution)/shard_map/all_to_all | solution.py:155

commit v2 on v1

--- a/solution.py
+++ b/solution.py
@@ -15,6 +15,10 @@
 LANES = 128
 BLOCKS = HALF // LANES
 ROWS = 4 * BLOCKS
+HOURS = 16
+SCALE = 1.0 / math.sqrt(BINS * HOURS)
+STEP = 4
+SPARE = 4
 AXES = ("z", "y", "x", "core")
 VMEM_LIMIT = 48 * 1024 * 1024
 
@@ -56,7 +60,7 @@
             send[peer, item] = white
 
 
-def pick_kernel(wanted, place, held, send):
+def pick_kernel(wanted, place, pairs, held, send, where):
     peers, sources, cap, hours = send.shape[:4]
     homes = held.shape[1] // hours
     base, source_step = place[0], place[1]
@@ -69,15 +73,23 @@
                 for hour in range(hours):
                     send[peer, source, c, hour] = held[source, hour * homes + station]
 
-
-def stack_kernel(first, second, count, slots, weights, series, sums, folded):
-    pairs, hours = sums.shape[0], slots.shape[1]
+    slot = pairs[...]
+    high, low, c = slot // (peers * cap), (slot // cap) % peers, slot % cap
+    turned = (low * sources + high) * cap + c
+    is_slot = lax.broadcasted_iota(jnp.int32, slot.shape, 0) < slot.shape[0] - SPARE
+    where[...] = jnp.where((place[2] == 1) & is_slot, turned, slot)
+
+
+def stack_kernel(pairs, slots, table, series, weights, sums, sem):
+    count, hours = sums.shape[0], slots.shape[1]
+    load = pltpu.make_async_copy(table, weights, sem)
+    load.start()
     place = lax.broadcasted_iota(jnp.int32, (BLOCKS, LANES), 0) + lax.broadcasted_iota(jnp.int32, (BLOCKS, LANES), 1)
     corner = place == 0
 
-    @pl.loop(0, pairs, unroll=8)
+    @pl.loop(0, count, unroll=16)
     def _(p):
-        a, b = first[p], second[p]
+        a, b = pairs[p], pairs[count + p]
         total_real, total_imag = 0.0, 0.0
         for hour in range(hours):
             left = slots[a, hour].astype(jnp.float32)
@@ -90,13 +102,16 @@
         sums[p, :BLOCKS] = low + high
         sums[p, BLOCKS:] = jnp.where(corner, low - high, total_imag[:BLOCKS] - total_imag[BLOCKS:])
 
-    live = lax.broadcasted_iota(jnp.int32, (pairs, LANES), 0) < count[0]
-    for j in range(2 * BLOCKS):
-        folded[:, j * LANES : (j + 1) * LANES] = jnp.where(live, sums[:, j, :], 0.0).astype(jnp.bfloat16)
-    for j in range(0, LAGS, 256):
-        series[:, j : j + 256] = jnp.dot(
-            folded[...], weights[:, j : j + 256], preferred_element_type=jnp.float32
-        ).astype(jnp.bfloat16)
+    live = lax.broadcasted_iota(jnp.int32, (count, LANES), 0) < pairs[2 * count]
+    load.wait()
+    total = None
+    for j in range(0, 2 * BLOCKS, STEP):
+        folded = jnp.concatenate(
+            [jnp.where(live, sums[:, j + i, :], 0.0).astype(jnp.bfloat16) for i in range(STEP)], axis=1
+        )
+        part = jnp.dot(folded, weights[j * LANES : (j + STEP) * LANES, :], preferred_element_type=jnp.float32)
+        total = part if total is None else total + part
+    series[...] = (total * SCALE).astype(jnp.bfloat16)
 
 
 def grid_groups(depth, height, width, cores):
@@ -126,9 +141,10 @@
     smem = pl.BlockSpec(memory_space=pltpu.SMEM)
     params = pltpu.CompilerParams(vmem_limit_bytes=VMEM_LIMIT)
 
-    wanted = lax.all_gather(
-        requests.reshape(1, tiles * cap), AXES, axis=0, axis_index_groups=stage_two, tiled=True
-    )
+    spot = jnp.where(core == 0, y, z)
+    row = lax.broadcasted_iota(jnp.int32, (side, tiles * cap), 0)
+    own = jnp.where(row == spot, requests.reshape(1, tiles * cap), 0)
+    wanted = lax.psum(own, AXES, axis_index_groups=stage_two)
     copies = pl.pallas_call(
         whiten_kernel,
         out_shape=jax.ShapeDtypeStruct((side, hours * homes, ROWS, LANES), jnp.bfloat16),
@@ -143,36 +159,36 @@
         [
             jnp.where(first_core, y * cap, z * height * cap),
             jnp.where(first_core, height * cap, cap),
+            jnp.where(first_core, 1, 0),
         ]
     )
-    send = pl.pallas_call(
+    spare = jnp.broadcast_to(pair_count, (SPARE * LANES,))
+    described = jnp.concatenate([pair_first, pair_second, spare]).reshape(-1, LANES)
+    send, where = pl.pallas_call(
         pick_kernel,
-        out_shape=jax.ShapeDtypeStruct((side, side, cap, hours, ROWS, LANES), jnp.bfloat16),
-        in_specs=[smem, smem, vmem],
-        out_specs=vmem,
+        out_shape=(
+            jax.ShapeDtypeStruct((side, side, cap, hours, ROWS, LANES), jnp.bfloat16),
+            jax.ShapeDtypeStruct(described.shape, jnp.int32),
+        ),
+        in_specs=[smem, smem, vmem, vmem],
+        out_specs=(vmem, vmem),
         compiler_params=params,
-    )(wanted, place, held)
+    )(wanted, place, described, held)
     slots = lax.all_to_all(send, AXES, 0, 0, axis_index_groups=stage_two, tiled=True)
-
-    def where_held(slot):
-        home, c = slot // cap, slot % cap
-        turned = ((home % height) * depth + home // height) * cap + c
-        return jnp.where(first_core, turned, slot)
-
     series = pl.pallas_call(
         stack_kernel,
         out_shape=jax.ShapeDtypeStruct((pairs, LAGS), jnp.bfloat16),
-        in_specs=[smem, smem, smem, vmem, vmem],
+        in_specs=[smem, vmem, pl.BlockSpec(memory_space=pl.ANY)],
         out_specs=vmem,
         scratch_shapes=[
+            pltpu.VMEM((BINS, LAGS), jnp.bfloat16),
             pltpu.VMEM((pairs, 2 * BLOCKS, LANES), jnp.float32),
-            pltpu.VMEM((pairs, BINS), jnp.bfloat16),
+            pltpu.SemaphoreType.DMA,
         ],
         compiler_params=params,
-    )(where_held(pair_first), where_held(pair_second), pair_count, slots.reshape(tiles * cap, hours, ROWS, LANES), table)
+    )(where.reshape(-1), slots.reshape(tiles * cap, hours, ROWS, LANES), table)
     parts = lax.all_to_all(series.reshape(windows, pairs // windows, LAGS), ("x", "core"), 0, 0, tiled=True)
-    scale = 1.0 / math.sqrt(BINS * hours * windows)
-    return jnp.sum(parts.astype(jnp.float32), axis=0) * scale
+    return jnp.sum(parts.astype(jnp.float32), axis=0)
 
 
 def solution(mesh):

time: 94 us -> 90.6 us (0.964)
  blocking collectives: 38.3 us -> 72.7 us
  waiting for transfers between devices: 28.7 us -> 0.01 us
  starting transfers between devices: 13.7 us -> 7.65 us
  Pallas kernels: 8.93 us -> 7.19 us
  local copies, waits for them, and re-layouts: 2.49 us -> 1.15 us
    all_to_all x0 -> x1, blocking collectives: none -> 38.8 us  [body(): lax.all_to_all(send, AXES, 0, 0, axis_index_groups=stage_two, tiled=True)]
    all_to_all x1 -> x0, waiting for transfers between devices: 28.7 us -> none  [body(): lax.all_to_all(send, AXES, 0, 0, axis_index_groups=stage_two, tiled=True)]
    all_gather x1 -> x0, blocking collectives: 21.6 us -> none  [body(): lax.all_gather(requests.reshape(1, tiles * cap), AXES, axis=0, axis_index...]
    psum x0 -> x1, blocking collectives: none -> 17 us  [body(): wanted = lax.psum(own, AXES, axis_index_groups=stage_two)]
    all_to_all x1 -> x0, starting transfers between devices: 6.09 us -> none  [body(): lax.all_to_all(send, AXES, 0, 0, axis_index_groups=stage_two, tiled=True)]
    pallas_call x1, Pallas kernels: 6.53 us -> 4.76 us  [body(): pl.pallas_call(stack_kernel, out_shape=jax.ShapeDtypeStruct((pairs, LAGS)...]
    unnamed x12 -> x9, local copies, waits for them, and re-layouts: 2.49 us -> 1.01 us
  transfers between devices with their start and end apart: 2 -> 1, of which waited for: 1 -> 0; matrix products, arithmetic and copies ran while one was open for 0% -> 0% of each run, Pallas kernels for 0% -> 0%
where the time goes in v2:
time: 90.6 us; the launch traced here: 90.3 us
  blocking collectives  72.7 us (80%)
  starting transfers between devices  7.65 us (8%)
  Pallas kernels  7.19 us (8%)
  local copies, waits for them, and re-layouts  1.15 us (1%)
    all_to_all x1, blocking collectives, body(): lax.all_to_all(send, AXES, 0, 0, axis_index_groups=stage_two, tiled=True)  38.8 us
    all_to_all x1, blocking collectives, body(): lax.all_to_all(series.reshape(windows, pairs // windows, LAGS), ('x', 'co...  17 us
    psum x1, blocking collectives, body(): wanted = lax.psum(own, AXES, axis_index_groups=stage_two)  17 us
    all_to_all x1, starting transfers between devices, body(): lax.all_to_all(copies, AXES, 0, 0, axis_index_groups=stage_one, tiled=True)  7.65 us
    pallas_call x1, Pallas kernels, body(): pl.pallas_call(stack_kernel, out_shape=jax.ShapeDtypeStruct((pairs, LAGS)...  4.76 us
  transfers between devices with their start and end apart: 1, of which 0 were waited for; matrix products, arithmetic and copies ran while one was open for 0% of the time, Pallas kernels for 0%

profile of v2, /device:TPU:1, one launch (start us, length us, event | category | flops | bytes accessed | tf_op | source)
XLA Modules:
  0.0 90.3 jit_solution(8439423737227728282)
XLA Ops:
  0.0 0.0 copy-start
  0.0 0.9 copy-done
  0.9 0.0 copy-start.1
  0.9 0.0 copy-start.2
  0.9 0.0 copy-start.3
  0.9 1.4 %shard_map.64 = bf16[8,16,32,128]{3,2,1,0:T(8,128)(2,1)} custom-call(bf16[2,8,4096]{2,1,0:T(8,128)(2,1)S(1)} %copy-done), custom_call_target="tpu_custom_call" | custom-call | tf_op jit(solution)/shard_map/pallas_call | solution.py:148
  2.4 7.7 %all-to-all-start = ((bf16[8,16,32,128]{3,2,1,0:T(8,128)(2,1)}), bf16[8,16,32,128]{3,2,1,0:T(8,128)(2,1)S(1)}, u32[]{:S(2)}, u32[]{:S(2)}) async-start(bf16[8,16,32,128]{3,2,1,0:T(8,128)(2,1)} %shard_map.64), calls=%async_computation | async-start | bytes 2097152 | tf_op jit(solution)/shard_map/all_to_all | solution.py:156
  10.7 0.0 copy-done.1
  10.7 0.1 copy.8
  10.8 0.1 broadcast_in_dim.21
  10.9 0.1 broadcast_select_fusion
  11.0 17.0 %psum.7.wanted = s32[8,128]{1,0:T(8,128)S(1)} all-reduce(s32[8,128]{1,0:T(8,128)S(1)} %broadcast_select_fusion), channel_id=1, replica_groups={{0,8,16,24,32,40,48,56},{2,10,18,26,34,42,50,58},{4,12,20,28,36,44,52,6..., use_global_device_ids=true, to_apply=%region_0.1 | all-reduce | flops 1024 | bytes 8192 | tf_op jit(solution)/shard_map/psum | solution.py:147
  27.9 0.1 pad_add_fusion.place
  28.0 0.0 copy-done.2
  28.0 0.0 copy-done.3
  28.0 0.0 all-to-all-done.held
  28.1 1.0 %shard_map.65 = (bf16[8,8,2,2,32,128]{5,4,3,2,1,0:T(8,128)(2,1)S(1)}, s32[8,128]{1,0:T(8,128)S(1)}) custom-call(s32[8,128]{1,0:T(8,128)S(1)} %psum.7.wanted, s32[3]{0:T(128)S(1)} %pad_add_fusion.place, s32[8,128]{1,0:T(8,128)S(1)} %add_bitcast_fusion.pairs, bf16[8,16,32,128]{3,2,1,0:T(8,128)(2,1)S(1)} %all-to-all-done.held), custom_call_target="tpu_custom_call" | custom-call | tf_op jit(solution)/shard_map/pallas_call | solution.py:167
  29.0 38.8 %all_to_all.15 = bf16[8,8,2,2,32,128]{5,4,3,2,1,0:T(8,128)(2,1)S(1)} all-to-all(bf16[8,8,2,2,32,128]{5,4,3,2,1,0:T(8,128)(2,1)S(1)} %get-tuple-element.8), channel_id=1, replica_groups={{0,8,16,24,32,40,48,56},{2,10,18,26,34,42,50,58},{4,12,20,28,36,44,52,6..., dimensions={0} | all-to-all | bytes 4194304 | tf_op jit(solution)/shard_map/all_to_all | solution.py:177
  67.8 4.8 %shard_map.66 = bf16[256,1024]{1,0:T(8,128)(2,1)S(1)} custom-call(s32[1024]{0:T(1024)S(1)} %bitcast.12, bf16[128,2,32,128]{3,2,1,0:T(8,128)(2,1)S(1)} %bitcast.10, bf16[2048,1024]{1,0:T(8,128)(2,1)} %constant.27.clone.table), custom_call_target="tpu_custom_call" | custom-call | tf_op jit(solution)/shard_map/pallas_call | solution.py:178
  72.6 17.0 %all_to_all.16 = bf16[8,32,1024]{2,1,0:T(8,128)(2,1)S(1)} all-to-all(bf16[8,32,1024]{2,1,0:T(8,128)(2,1)S(1)} %bitcast.11), channel_id=1, replica_groups=mesh['z'=8,'y'=8,'x'=4,'core'=2] {'x','core'}, dimensions={0} | all-to-all | bytes 1048576 | tf_op jit(solution)/shard_map/all_to_all | solution.py:190
  89.6 0.7 convert_reduce_fusion
  (3 shorter events, 0.0 us)
Async XLA Ops:
  0.0 0.9 %copy-start = (bf16[2,8,4096]{2,1,0:T(8,128)(2,1)S(1)}, bf16[2,8,4096]{2,1,0:T(8,128)(2,1)}, u32[]{:S(2)}) copy-start(bf16[2,8,4096]{2,1,0:T(8,128)(2,1)} %spectra.1) | copy-start | bytes 393220
  0.9 9.8 %copy-start.1 = (s32[1,64,2]{1,2,0:T(2,128)S(1)}, s32[1,64,2]{1,2,0:T(2,128)}, u32[]{:S(2)}) copy-start(s32[1,64,2]{1,2,0:T(2,128)} %param.7) | copy-start | bytes 1540
  0.9 27.1 %copy-start.2 = (s32[256]{0:T(256)S(1)}, s32[256]{0:T(256)}, u32[]{:S(2)}) copy-start(s32[256]{0:T(256)} %param.9) | copy-start | bytes 3076
  0.9 27.1 %copy-start.3 = (s32[256]{0:T(256)S(1)}, s32[256]{0:T(256)}, u32[]{:S(2)}) copy-start(s32[256]{0:T(256)} %param.8) | copy-start | bytes 3076
  2.4 25.7 %all-to-all-start = ((bf16[8,16,32,128]{3,2,1,0:T(8,128)(2,1)}), bf16[8,16,32,128]{3,2,1,0:T(8,128)(2,1)S(1)}, u32[]{:S(2)}, u32[]{:S(2)}) async-start(bf16[8,16,32,128]{3,2,1,0:T(8,128)(2,1)} %shard_map.64), calls=%async_computation | async-start | bytes 2097152 | tf_op jit(solution)/shard_map/all_to_all | solution.py:156

commit v3 on v2

--- a/solution.py
+++ b/solution.py
@@ -17,10 +17,10 @@
 ROWS = 4 * BLOCKS
 HOURS = 16
 SCALE = 1.0 / math.sqrt(BINS * HOURS)
-STEP = 4
+STEP = 2
 SPARE = 4
 AXES = ("z", "y", "x", "core")
-VMEM_LIMIT = 48 * 1024 * 1024
+VMEM_LIMIT = 16 * 1024 * 1024
 
 
 def fold_table():
@@ -65,11 +65,11 @@
     homes = held.shape[1] // hours
     base, source_step = place[0], place[1]
 
-    @pl.loop(0, peers)
+    @pl.loop(0, peers, unroll=2)
     def _(peer):
         for source in range(sources):
             for c in range(cap):
-                station = wanted[peer, base + source * source_step + c]
+                station = wanted[peer, c, base + source * source_step]
                 for hour in range(hours):
                     send[peer, source, c, hour] = held[source, hour * homes + station]
 
@@ -80,10 +80,8 @@
     where[...] = jnp.where((place[2] == 1) & is_slot, turned, slot)
 
 
-def stack_kernel(pairs, slots, table, series, weights, sums, sem):
+def stack_kernel(pairs, slots, weights, series, sums):
     count, hours = sums.shape[0], slots.shape[1]
-    load = pltpu.make_async_copy(table, weights, sem)
-    load.start()
     place = lax.broadcasted_iota(jnp.int32, (BLOCKS, LANES), 0) + lax.broadcasted_iota(jnp.int32, (BLOCKS, LANES), 1)
     corner = place == 0
 
@@ -103,7 +101,6 @@
         sums[p, BLOCKS:] = jnp.where(corner, low - high, total_imag[:BLOCKS] - total_imag[BLOCKS:])
 
     live = lax.broadcasted_iota(jnp.int32, (count, LANES), 0) < pairs[2 * count]
-    load.wait()
     total = None
     for j in range(0, 2 * BLOCKS, STEP):
         folded = jnp.concatenate(
@@ -142,8 +139,8 @@
     params = pltpu.CompilerParams(vmem_limit_bytes=VMEM_LIMIT)
 
     spot = jnp.where(core == 0, y, z)
-    row = lax.broadcasted_iota(jnp.int32, (side, tiles * cap), 0)
-    own = jnp.where(row == spot, requests.reshape(1, tiles * cap), 0)
+    row = lax.broadcasted_iota(jnp.int32, (side, cap, tiles), 0)
+    own = jnp.where(row == spot, jnp.transpose(requests, (0, 2, 1)), 0)
     wanted = lax.psum(own, AXES, axis_index_groups=stage_two)
     copies = pl.pallas_call(
         whiten_kernel,
@@ -157,8 +154,8 @@
     first_core = core == 0
     place = jnp.stack(
         [
-            jnp.where(first_core, y * cap, z * height * cap),
-            jnp.where(first_core, height * cap, cap),
+            jnp.where(first_core, y, z * height),
+            jnp.where(first_core, height, 1),
             jnp.where(first_core, 1, 0),
         ]
     )
@@ -178,13 +175,9 @@
     series = pl.pallas_call(
         stack_kernel,
         out_shape=jax.ShapeDtypeStruct((pairs, LAGS), jnp.bfloat16),
-        in_specs=[smem, vmem, pl.BlockSpec(memory_space=pl.ANY)],
+        in_specs=[smem, vmem, vmem],
         out_specs=vmem,
-        scratch_shapes=[
-            pltpu.VMEM((BINS, LAGS), jnp.bfloat16),
-            pltpu.VMEM((pairs, 2 * BLOCKS, LANES), jnp.float32),
-            pltpu.SemaphoreType.DMA,
-        ],
+        scratch_shapes=[pltpu.VMEM((pairs, 2 * BLOCKS, LANES), jnp.float32)],
         compiler_params=params,
     )(where.reshape(-1), slots.reshape(tiles * cap, hours, ROWS, LANES), table)
     parts = lax.all_to_all(series.reshape(windows, pairs // windows, LAGS), ("x", "core"), 0, 0, tiled=True)

time: 90.6 us -> 90.5 us (level)
  no operation moved by 1% of the time
where the time goes in v3:
time: 90.5 us; the launch traced here: 90.3 us
  blocking collectives  73.4 us (81%)
  starting transfers between devices  7.65 us (8%)
  Pallas kernels  6.7 us (7%)
  local copies, waits for them, and re-layouts  0.92 us (1%)
    all_to_all x1, blocking collectives, body(): lax.all_to_all(send, AXES, 0, 0, axis_index_groups=stage_two, tiled=True)  39.1 us
    psum x1, blocking collectives, body(): wanted = lax.psum(own, AXES, axis_index_groups=stage_two)  17.3 us
    all_to_all x1, blocking collectives, body(): lax.all_to_all(series.reshape(windows, pairs // windows, LAGS), ('x', 'co...  17 us
    all_to_all x1, starting transfers between devices, body(): lax.all_to_all(copies, AXES, 0, 0, axis_index_groups=stage_one, tiled=True)  7.65 us
    pallas_call x1, Pallas kernels, body(): pl.pallas_call(stack_kernel, out_shape=jax.ShapeDtypeStruct((pairs, LAGS)...  4.27 us
  transfers between devices with their start and end apart: 1, of which 0 were waited for; matrix products, arithmetic and copies ran while one was open for 0% of the time, Pallas kernels for 0%

profile of v3, /device:TPU:1, one launch (start us, length us, event | category | flops | bytes accessed | tf_op | source)
XLA Modules:
  0.0 90.3 jit_solution(1055576369501299392)
XLA Ops:
  0.0 0.0 copy-start.1
  0.0 0.9 copy-done.1
  0.9 0.0 copy-start.2
  0.9 0.0 copy-start.3
  0.9 0.0 copy-start.4
  0.9 1.4 %shard_map.64 = bf16[8,16,32,128]{3,2,1,0:T(8,128)(2,1)} custom-call(bf16[2,8,4096]{2,1,0:T(8,128)(2,1)S(1)} %copy-done.1), custom_call_target="tpu_custom_call" | custom-call | tf_op jit(solution)/shard_map/pallas_call | solution.py:145
  2.4 7.7 %all-to-all-start = ((bf16[8,16,32,128]{3,2,1,0:T(8,128)(2,1)}), bf16[8,16,32,128]{3,2,1,0:T(8,128)(2,1)S(1)}, u32[]{:S(2)}, u32[]{:S(2)}) async-start(bf16[8,16,32,128]{3,2,1,0:T(8,128)(2,1)} %shard_map.64), calls=%async_computation | async-start | bytes 2097152 | tf_op jit(solution)/shard_map/all_to_all | solution.py:153
  10.7 0.0 copy-done.2
  10.7 0.1 broadcast_select_fusion
  10.8 17.3 %psum.7.wanted = s32[8,2,64]{2,1,0:T(2,128)S(1)} all-reduce(s32[8,2,64]{2,1,0:T(2,128)S(1)} %broadcast_select_fusion), channel_id=1, replica_groups={{0,8,16,24,32,40,48,56},{2,10,18,26,34,42,50,58},{4,12,20,28,36,44,52,6..., use_global_device_ids=true, to_apply=%region_0.1 | all-reduce | flops 1024 | bytes 8192 | tf_op jit(solution)/shard_map/psum | solution.py:144
  28.0 0.1 pad_add_fusion.place
  28.1 0.0 copy-done.3
  28.1 0.0 copy-done.4
  28.1 0.0 all-to-all-done.held
  28.2 1.0 %shard_map.65 = (bf16[8,8,2,2,32,128]{5,4,3,2,1,0:T(8,128)(2,1)S(1)}, s32[8,128]{1,0:T(8,128)S(1)}) custom-call(s32[8,2,64]{2,1,0:T(2,128)S(1)} %psum.7.wanted, s32[3]{0:T(128)S(1)} %pad_add_fusion.place, s32[8,128]{1,0:T(8,128)S(1)} %add_bitcast_fusion.pairs, bf16[8,16,32,128]{3,2,1,0:T(8,128)(2,1)S(1)} %all-to-all-done.held), custom_call_target="tpu_custom_call" | custom-call | tf_op jit(solution)/shard_map/pallas_call | solution.py:164
  29.2 0.0 copy-start
  29.2 39.1 %all_to_all.15 = bf16[8,8,2,2,32,128]{5,4,3,2,1,0:T(8,128)(2,1)S(1)} all-to-all(bf16[8,8,2,2,32,128]{5,4,3,2,1,0:T(8,128)(2,1)S(1)} %get-tuple-element.8), channel_id=1, replica_groups={{0,8,16,24,32,40,48,56},{2,10,18,26,34,42,50,58},{4,12,20,28,36,44,52,6..., dimensions={0} | all-to-all | bytes 4194304 | tf_op jit(solution)/shard_map/all_to_all | solution.py:174
  68.3 0.0 copy-done
  68.3 4.3 %shard_map.66 = bf16[256,1024]{1,0:T(8,128)(2,1)S(1)} custom-call(s32[1024]{0:T(1024)S(1)} %bitcast.15, bf16[128,2,32,128]{3,2,1,0:T(8,128)(2,1)S(1)} %bitcast.13, bf16[2048,1024]{1,0:T(8,128)(2,1)S(1)} %copy-done), custom_call_target="tpu_custom_call" | custom-call | tf_op jit(solution)/shard_map/pallas_call | solution.py:175
  72.5 17.0 %all_to_all.16 = bf16[8,32,1024]{2,1,0:T(8,128)(2,1)S(1)} all-to-all(bf16[8,32,1024]{2,1,0:T(8,128)(2,1)S(1)} %bitcast.14), channel_id=1, replica_groups=mesh['z'=8,'y'=8,'x'=4,'core'=2] {'x','core'}, dimensions={0} | all-to-all | bytes 1048576 | tf_op jit(solution)/shard_map/all_to_all | solution.py:183
  89.5 0.7 convert_reduce_fusion
  (3 shorter events, 0.0 us)
Async XLA Ops:
  0.0 0.9 %copy-start.1 = (bf16[2,8,4096]{2,1,0:T(8,128)(2,1)S(1)}, bf16[2,8,4096]{2,1,0:T(8,128)(2,1)}, u32[]{:S(2)}) copy-start(bf16[2,8,4096]{2,1,0:T(8,128)(2,1)} %spectra.1) | copy-start | bytes 393220
  0.9 9.8 %copy-start.2 = (s32[1,64,2]{1,2,0:T(2,128)S(1)}, s32[1,64,2]{1,2,0:T(2,128)}, u32[]{:S(2)}) copy-start(s32[1,64,2]{1,2,0:T(2,128)} %param.7) | copy-start | bytes 1540
  0.9 27.2 %copy-start.3 = (s32[256]{0:T(256)S(1)}, s32[256]{0:T(256)}, u32[]{:S(2)}) copy-start(s32[256]{0:T(256)} %param.9) | copy-start | bytes 3076
  0.9 27.2 %copy-start.4 = (s32[256]{0:T(256)S(1)}, s32[256]{0:T(256)}, u32[]{:S(2)}) copy-start(s32[256]{0:T(256)} %param.8) | copy-start | bytes 3076
  2.4 25.8 %all-to-all-start = ((bf16[8,16,32,128]{3,2,1,0:T(8,128)(2,1)}), bf16[8,16,32,128]{3,2,1,0:T(8,128)(2,1)S(1)}, u32[]{:S(2)}, u32[]{:S(2)}) async-start(bf16[8,16,32,128]{3,2,1,0:T(8,128)(2,1)} %shard_map.64), calls=%async_computation | async-start | bytes 2097152 | tf_op jit(solution)/shard_map/all_to_all | solution.py:153
  29.2 39.1 %copy-start = (bf16[2048,1024]{1,0:T(8,128)(2,1)S(1)}, bf16[2048,1024]{1,0:T(8,128)(2,1)}, u32[]{:S(2)}) copy-start(bf16[2048,1024]{1,0:T(8,128)(2,1)} %constant.23.clone.weights) | copy-start | bytes 12582916

commit v4 on v3

--- a/solution.py
+++ b/solution.py
@@ -60,13 +60,14 @@
             send[peer, item] = white
 
 
-def pick_kernel(wanted, place, pairs, held, send, where):
+def pick_kernel(wanted, pairs, held, send, where):
     peers, sources, cap, hours = send.shape[:4]
     homes = held.shape[1] // hours
-    base, source_step = place[0], place[1]
+    first_core = lax.axis_index("core") == 0
+    base = jnp.where(first_core, lax.axis_index("y"), lax.axis_index("z") * peers)
+    source_step = jnp.where(first_core, peers, 1)
 
-    @pl.loop(0, peers, unroll=2)
-    def _(peer):
+    for peer in range(peers):
         for source in range(sources):
             for c in range(cap):
                 station = wanted[peer, c, base + source * source_step]
@@ -77,7 +78,7 @@
     high, low, c = slot // (peers * cap), (slot // cap) % peers, slot % cap
     turned = (low * sources + high) * cap + c
     is_slot = lax.broadcasted_iota(jnp.int32, slot.shape, 0) < slot.shape[0] - SPARE
-    where[...] = jnp.where((place[2] == 1) & is_slot, turned, slot)
+    where[...] = jnp.where(first_core & is_slot, turned, slot)
 
 
 def stack_kernel(pairs, slots, weights, series, sums):
@@ -151,14 +152,6 @@
         compiler_params=params,
     )(spectra)
     held = lax.all_to_all(copies, AXES, 0, 0, axis_index_groups=stage_one, tiled=True)
-    first_core = core == 0
-    place = jnp.stack(
-        [
-            jnp.where(first_core, y, z * height),
-            jnp.where(first_core, height, 1),
-            jnp.where(first_core, 1, 0),
-        ]
-    )
     spare = jnp.broadcast_to(pair_count, (SPARE * LANES,))
     described = jnp.concatenate([pair_first, pair_second, spare]).reshape(-1, LANES)
     send, where = pl.pallas_call(
@@ -167,10 +160,10 @@
             jax.ShapeDtypeStruct((side, side, cap, hours, ROWS, LANES), jnp.bfloat16),
             jax.ShapeDtypeStruct(described.shape, jnp.int32),
         ),
-        in_specs=[smem, smem, vmem, vmem],
+        in_specs=[smem, vmem, vmem],
         out_specs=(vmem, vmem),
         compiler_params=params,
-    )(wanted, place, described, held)
+    )(wanted, described, held)
     slots = lax.all_to_all(send, AXES, 0, 0, axis_index_groups=stage_two, tiled=True)
     series = pl.pallas_call(
         stack_kernel,

time: 90.5 us -> 90.4 us (level)
  no operation moved by 1% of the time
where the time goes in v4:
time: 90.4 us; the launch traced here: 90.2 us
  blocking collectives  73.4 us (81%)
  starting transfers between devices  7.65 us (8%)
  Pallas kernels  6.6 us (7%)
  local copies, waits for them, and re-layouts  0.92 us (1%)
    all_to_all x1, blocking collectives, body(): lax.all_to_all(send, AXES, 0, 0, axis_index_groups=stage_two, tiled=True)  39.2 us
    psum x1, blocking collectives, body(): wanted = lax.psum(own, AXES, axis_index_groups=stage_two)  17.3 us
    all_to_all x1, blocking collectives, body(): lax.all_to_all(series.reshape(windows, pairs // windows, LAGS), ('x', 'co...  17 us
    all_to_all x1, starting transfers between devices, body(): lax.all_to_all(copies, AXES, 0, 0, axis_index_groups=stage_one, tiled=True)  7.65 us
    pallas_call x1, Pallas kernels, body(): pl.pallas_call(stack_kernel, out_shape=jax.ShapeDtypeStruct((pairs, LAGS)...  4.26 us
  transfers between devices with their start and end apart: 1, of which 0 were waited for; matrix products, arithmetic and copies ran while one was open for 0% of the time, Pallas kernels for 0%

profile of v4, /device:TPU:1, one launch (start us, length us, event | category | flops | bytes accessed | tf_op | source)
XLA Modules:
  0.0 90.2 jit_solution(14071994563135823181)
XLA Ops:
  0.0 0.0 copy-start.1
  0.0 0.9 %copy-done.1 = bf16[2,8,4096]{2,1,0:T(8,128)(2,1)S(1)} copy-done((bf16[2,8,4096]{2,1,0:T(8,128)(2,1)S(1)}, bf16[2,8,4096]{2,1,0:T(8,128)(2,1)}, u32[]{:S(2)}) %copy-start.1) | copy-done | bytes 131096
  0.9 0.0 copy-start.2
  0.9 0.0 copy-start.3
  0.9 0.0 copy-start.4
  0.9 1.4 %shard_map.64 = bf16[8,16,32,128]{3,2,1,0:T(8,128)(2,1)} custom-call(bf16[2,8,4096]{2,1,0:T(8,128)(2,1)S(1)} %copy-done.1), custom_call_target="tpu_custom_call" | custom-call | tf_op jit(solution)/shard_map/pallas_call | solution.py:146
  2.4 7.7 %all-to-all-start = ((bf16[8,16,32,128]{3,2,1,0:T(8,128)(2,1)}), bf16[8,16,32,128]{3,2,1,0:T(8,128)(2,1)S(1)}, u32[]{:S(2)}, u32[]{:S(2)}) async-start(bf16[8,16,32,128]{3,2,1,0:T(8,128)(2,1)} %shard_map.64), calls=%async_computation | async-start | bytes 2097152 | tf_op jit(solution)/shard_map/all_to_all | solution.py:154
  10.7 0.0 copy-done.2
  10.7 0.1 broadcast_select_fusion
  10.8 17.3 %psum.7.wanted = s32[8,2,64]{2,1,0:T(2,128)S(1)} all-reduce(s32[8,2,64]{2,1,0:T(2,128)S(1)} %broadcast_select_fusion), channel_id=1, replica_groups={{0,8,16,24,32,40,48,56},{2,10,18,26,34,42,50,58},{4,12,20,28,36,44,52,6..., use_global_device_ids=true, to_apply=%region_0.1 | all-reduce | flops 1024 | bytes 8192 | tf_op jit(solution)/shard_map/psum | solution.py:145
  28.0 0.0 copy-done.3
  28.1 0.0 copy-done.4
  28.1 0.0 all-to-all-done.held
  28.1 0.9 shard_map.65
  29.0 0.0 copy-start
  29.0 39.2 %all_to_all.15 = bf16[8,8,2,2,32,128]{5,4,3,2,1,0:T(8,128)(2,1)S(1)} all-to-all(bf16[8,8,2,2,32,128]{5,4,3,2,1,0:T(8,128)(2,1)S(1)} %get-tuple-element.8), channel_id=1, replica_groups={{0,8,16,24,32,40,48,56},{2,10,18,26,34,42,50,58},{4,12,20,28,36,44,52,6..., dimensions={0} | all-to-all | bytes 4194304 | tf_op jit(solution)/shard_map/all_to_all | solution.py:167
  68.2 0.0 copy-done
  68.2 4.3 %shard_map.66 = bf16[256,1024]{1,0:T(8,128)(2,1)S(1)} custom-call(s32[1024]{0:T(1024)S(1)} %bitcast.12, bf16[128,2,32,128]{3,2,1,0:T(8,128)(2,1)S(1)} %bitcast.10, bf16[2048,1024]{1,0:T(8,128)(2,1)S(1)} %copy-done), custom_call_target="tpu_custom_call" | custom-call | tf_op jit(solution)/shard_map/pallas_call | solution.py:168
  72.4 17.0 %all_to_all.16 = bf16[8,32,1024]{2,1,0:T(8,128)(2,1)S(1)} all-to-all(bf16[8,32,1024]{2,1,0:T(8,128)(2,1)S(1)} %bitcast.11), channel_id=1, replica_groups=mesh['z'=8,'y'=8,'x'=4,'core'=2] {'x','core'}, dimensions={0} | all-to-all | bytes 1048576 | tf_op jit(solution)/shard_map/all_to_all | solution.py:176
  89.4 0.7 convert_reduce_fusion
  (3 shorter events, 0.0 us)
Async XLA Ops:
  0.0 0.9 %copy-start.1 = (bf16[2,8,4096]{2,1,0:T(8,128)(2,1)S(1)}, bf16[2,8,4096]{2,1,0:T(8,128)(2,1)}, u32[]{:S(2)}) copy-start(bf16[2,8,4096]{2,1,0:T(8,128)(2,1)} %spectra.1) | copy-start | bytes 393220
  0.9 9.8 %copy-start.2 = (s32[1,64,2]{1,2,0:T(2,128)S(1)}, s32[1,64,2]{1,2,0:T(2,128)}, u32[]{:S(2)}) copy-start(s32[1,64,2]{1,2,0:T(2,128)} %param.7) | copy-start | bytes 1540
  0.9 27.1 %copy-start.3 = (s32[256]{0:T(256)S(1)}, s32[256]{0:T(256)}, u32[]{:S(2)}) copy-start(s32[256]{0:T(256)} %param.9) | copy-start | bytes 3076
  0.9 27.1 %copy-start.4 = (s32[256]{0:T(256)S(1)}, s32[256]{0:T(256)}, u32[]{:S(2)}) copy-start(s32[256]{0:T(256)} %param.8) | copy-start | bytes 3076
  2.4 25.7 %all-to-all-start = ((bf16[8,16,32,128]{3,2,1,0:T(8,128)(2,1)}), bf16[8,16,32,128]{3,2,1,0:T(8,128)(2,1)S(1)}, u32[]{:S(2)}, u32[]{:S(2)}) async-start(bf16[8,16,32,128]{3,2,1,0:T(8,128)(2,1)} %shard_map.64), calls=%async_computation | async-start | bytes 2097152 | tf_op jit(solution)/shard_map/all_to_all | solution.py:154
  29.0 39.2 %copy-start = (bf16[2048,1024]{1,0:T(8,128)(2,1)S(1)}, bf16[2048,1024]{1,0:T(8,128)(2,1)}, u32[]{:S(2)}) copy-start(bf16[2048,1024]{1,0:T(8,128)(2,1)} %constant.19.clone.weights) | copy-start | bytes 12582916

commit v5 on v4

--- a/solution.py
+++ b/solution.py
@@ -1,3 +1,4 @@
+import functools
 import math
 
 import jax
@@ -81,7 +82,7 @@
     where[...] = jnp.where(first_core & is_slot, turned, slot)
 
 
-def stack_kernel(pairs, slots, weights, series, sums):
+def stack_kernel(owned, pairs, slots, weights, mine, theirs, sums):
     count, hours = sums.shape[0], slots.shape[1]
     place = lax.broadcasted_iota(jnp.int32, (BLOCKS, LANES), 0) + lax.broadcasted_iota(jnp.int32, (BLOCKS, LANES), 1)
     corner = place == 0
@@ -109,7 +110,14 @@
         )
         part = jnp.dot(folded, weights[j * LANES : (j + STEP) * LANES, :], preferred_element_type=jnp.float32)
         total = part if total is None else total + part
-    series[...] = (total * SCALE).astype(jnp.bfloat16)
+    total = total * SCALE
+    core = lax.axis_index("core")
+    for block in range(count // (2 * owned)):
+        first = total[2 * block * owned : (2 * block + 1) * owned]
+        second = total[(2 * block + 1) * owned : (2 * block + 2) * owned]
+        rows = slice(block * owned, (block + 1) * owned)
+        mine[rows] = jnp.where(core == 0, first, second)
+        theirs[rows] = jnp.where(core == 0, second, first).astype(theirs.dtype)
 
 
 def grid_groups(depth, height, width, cores):
@@ -165,15 +173,20 @@
         compiler_params=params,
     )(wanted, described, held)
     slots = lax.all_to_all(send, AXES, 0, 0, axis_index_groups=stage_two, tiled=True)
-    series = pl.pallas_call(
-        stack_kernel,
-        out_shape=jax.ShapeDtypeStruct((pairs, LAGS), jnp.bfloat16),
+    owned = pairs // windows
+
+    half = (pairs // cores, LAGS)
+    ours, others = pl.pallas_call(
+        functools.partial(stack_kernel, owned),
+        out_shape=(jax.ShapeDtypeStruct(half, jnp.float32), jax.ShapeDtypeStruct(half, jnp.bfloat16)),
         in_specs=[smem, vmem, vmem],
-        out_specs=vmem,
+        out_specs=(vmem, vmem),
         scratch_shapes=[pltpu.VMEM((pairs, 2 * BLOCKS, LANES), jnp.float32)],
         compiler_params=params,
     )(where.reshape(-1), slots.reshape(tiles * cap, hours, ROWS, LANES), table)
-    parts = lax.all_to_all(series.reshape(windows, pairs // windows, LAGS), ("x", "core"), 0, 0, tiled=True)
+    theirs = lax.ppermute(others, "core", [(0, 1), (1, 0)])
+    both = (ours + theirs.astype(jnp.float32)).astype(jnp.bfloat16)
+    parts = lax.all_to_all(both.reshape(width, owned, LAGS), "x", 0, 0, tiled=True)
     return jnp.sum(parts.astype(jnp.float32), axis=0)
 
 

time: 90.4 us -> 89.6 us (level)
  blocking collectives: 73.4 us -> 66.1 us
  starting transfers between devices: 7.65 us -> 13.1 us
  waiting for transfers between devices: 0.01 us -> 1.14 us
    all_to_all x1, blocking collectives: 17 us -> 9.62 us  [body(): lax.all_to_all(both.reshape(width, owned, LAGS), 'x', 0, 0, tiled=True)]
    ppermute x0 -> x1, starting transfers between devices: none -> 5.45 us  [body(): theirs = lax.ppermute(others, 'core', [(0, 1), (1, 0)])]
    ppermute x0 -> x1, waiting for transfers between devices: none -> 1.14 us  [body(): theirs = lax.ppermute(others, 'core', [(0, 1), (1, 0)])]
  transfers between devices with their start and end apart: 1 -> 2, of which waited for: 0 -> 1; matrix products, arithmetic and copies ran while one was open for 0% -> 0% of each run, Pallas kernels for 0% -> 0%
where the time goes in v5:
time: 89.6 us; the launch traced here: 89.4 us
  blocking collectives  66.1 us (74%)
  starting transfers between devices  13.1 us (15%)
  Pallas kernels  6.59 us (7%)
  waiting for transfers between devices  1.14 us (1%)
  local copies, waits for them, and re-layouts  0.92 us (1%)
    all_to_all x1, blocking collectives, body(): lax.all_to_all(send, AXES, 0, 0, axis_index_groups=stage_two, tiled=True)  39.2 us
    psum x1, blocking collectives, body(): wanted = lax.psum(own, AXES, axis_index_groups=stage_two)  17.3 us
    all_to_all x1, blocking collectives, body(): lax.all_to_all(both.reshape(width, owned, LAGS), 'x', 0, 0, tiled=True)  9.62 us
    all_to_all x1, starting transfers between devices, body(): lax.all_to_all(copies, AXES, 0, 0, axis_index_groups=stage_one, tiled=True)  7.65 us
    ppermute x1, starting transfers between devices, body(): theirs = lax.ppermute(others, 'core', [(0, 1), (1, 0)])  5.45 us
    pallas_call x1, Pallas kernels, body(): pl.pallas_call(functools.partial(stack_kernel, owned), out_shape=(jax.Sha...  4.26 us
  transfers between devices with their start and end apart: 2, of which 1 were waited for; matrix products, arithmetic and copies ran while one was open for 0% of the time, Pallas kernels for 0%

profile of v5, /device:TPU:1, one launch (start us, length us, event | category | flops | bytes accessed | tf_op | source)
XLA Modules:
  0.0 89.4 jit_solution(13204929806886059863)
XLA Ops:
  0.0 0.0 copy-start.1
  0.0 0.9 %copy-done.1 = bf16[2,8,4096]{2,1,0:T(8,128)(2,1)S(1)} copy-done((bf16[2,8,4096]{2,1,0:T(8,128)(2,1)S(1)}, bf16[2,8,4096]{2,1,0:T(8,128)(2,1)}, u32[]{:S(2)}) %copy-start.1) | copy-done | bytes 131096
  0.9 0.0 copy-start.2
  0.9 0.0 copy-start.3
  0.9 0.0 copy-start.4
  0.9 1.4 %shard_map.64 = bf16[8,16,32,128]{3,2,1,0:T(8,128)(2,1)} custom-call(bf16[2,8,4096]{2,1,0:T(8,128)(2,1)S(1)} %copy-done.1), custom_call_target="tpu_custom_call" | custom-call | tf_op jit(solution)/shard_map/pallas_call | solution.py:154
  2.3 7.7 %all-to-all-start = ((bf16[8,16,32,128]{3,2,1,0:T(8,128)(2,1)}), bf16[8,16,32,128]{3,2,1,0:T(8,128)(2,1)S(1)}, u32[]{:S(2)}, u32[]{:S(2)}) async-start(bf16[8,16,32,128]{3,2,1,0:T(8,128)(2,1)} %shard_map.64), calls=%async_computation | async-start | bytes 2097152 | tf_op jit(solution)/shard_map/all_to_all | solution.py:162
  10.7 0.0 copy-done.2
  10.7 0.1 broadcast_select_fusion
  10.7 17.3 %psum.7.wanted = s32[8,2,64]{2,1,0:T(2,128)S(1)} all-reduce(s32[8,2,64]{2,1,0:T(2,128)S(1)} %broadcast_select_fusion), channel_id=1, replica_groups={{0,8,16,24,32,40,48,56},{2,10,18,26,34,42,50,58},{4,12,20,28,36,44,52,6..., use_global_device_ids=true, to_apply=%region_0.1 | all-reduce | flops 1024 | bytes 8192 | tf_op jit(solution)/shard_map/psum | solution.py:153
  28.0 0.0 copy-done.3
  28.1 0.0 copy-done.4
  28.1 0.0 all-to-all-done.held
  28.1 0.9 %shard_map.65 = (bf16[8,8,2,2,32,128]{5,4,3,2,1,0:T(8,128)(2,1)S(1)}, s32[8,128]{1,0:T(8,128)S(1)}) custom-call(s32[8,2,64]{2,1,0:T(2,128)S(1)} %psum.7.wanted, s32[8,128]{1,0:T(8,128)S(1)} %add_bitcast_fusion.pairs, bf16[8,16,32,128]{3,2,1,0:T(8,128)(2,1)S(1)} %all-to-all-done.held), custom_call_target="tpu_custom_call" | custom-call | tf_op jit(solution)/shard_map/pallas_call | solution.py:165
  29.0 0.0 copy-start
  29.0 39.2 %all_to_all.15 = bf16[8,8,2,2,32,128]{5,4,3,2,1,0:T(8,128)(2,1)S(1)} all-to-all(bf16[8,8,2,2,32,128]{5,4,3,2,1,0:T(8,128)(2,1)S(1)} %get-tuple-element.10), channel_id=1, replica_groups={{0,8,16,24,32,40,48,56},{2,10,18,26,34,42,50,58},{4,12,20,28,36,44,52,6..., dimensions={0} | all-to-all | bytes 4194304 | tf_op jit(solution)/shard_map/all_to_all | solution.py:175
  68.2 0.0 copy-done
  68.2 4.3 %shard_map.66 = (f32[128,1024]{1,0:T(8,128)S(1)}, bf16[128,1024]{1,0:T(8,128)(2,1)S(1)}) custom-call(s32[1024]{0:T(1024)S(1)} %bitcast.11, bf16[128,2,32,128]{3,2,1,0:T(8,128)(2,1)S(1)} %bitcast.10, bf16[2048,1024]{1,0:T(8,128)(2,1)S(1)} %copy-done), custom_call_target="tpu_custom_call" | custom-call | tf_op jit(solution)/shard_map/pallas_call | solution.py:179
  72.4 5.4 %collective-permute-start = (bf16[128,1024]{1,0:T(8,128)(2,1)S(1)}, bf16[128,1024]{1,0:T(8,128)(2,1)S(1)}, u32[]{:S(2)}, u32[]{:S(2)}) collective-permute-start(bf16[128,1024]{1,0:T(8,128)(2,1)S(1)} %get-tuple-element.12), channel_id=1, source_target_pairs={{0,1},{1,0},{2,3},{3,2},{4,5},{5,4},{6,7},{7,6},{8,9},{9,8},{10,11... | collective-permute-start | bytes 786440 | tf_op jit(solution)/shard_map/ppermute | solution.py:187
  77.9 1.1 %collective-permute-done = bf16[128,1024]{1,0:T(8,128)(2,1)S(1)} collective-permute-done((bf16[128,1024]{1,0:T(8,128)(2,1)S(1)}, bf16[128,1024]{1,0:T(8,128)(2,1)S(1)}, u32[]{:S(2)}, u32[]{:S(2)}) %collective-permute-start) | collective-permute-done | bytes 262176 | tf_op jit(solution)/shard_map/ppermute | solution.py:187
  79.0 0.1 add_convert_fusion
  79.1 9.6 %all_to_all.16 = bf16[4,32,1024]{2,1,0:T(8,128)(2,1)S(1)} all-to-all(bf16[4,32,1024]{2,1,0:T(8,128)(2,1)S(1)} %bitcast.12), channel_id=1, replica_groups=mesh['z'=8,'y'=8,'x'=4,'core'=2] {'x'}, dimensions={0} | all-to-all | bytes 524288 | tf_op jit(solution)/shard_map/all_to_all | solution.py:189
  88.7 0.7 convert_reduce_fusion
  (3 shorter events, 0.0 us)
Async XLA Ops:
  0.0 0.9 %copy-start.1 = (bf16[2,8,4096]{2,1,0:T(8,128)(2,1)S(1)}, bf16[2,8,4096]{2,1,0:T(8,128)(2,1)}, u32[]{:S(2)}) copy-start(bf16[2,8,4096]{2,1,0:T(8,128)(2,1)} %spectra.1) | copy-start | bytes 393220
  0.9 9.8 %copy-start.2 = (s32[1,64,2]{1,2,0:T(2,128)S(1)}, s32[1,64,2]{1,2,0:T(2,128)}, u32[]{:S(2)}) copy-start(s32[1,64,2]{1,2,0:T(2,128)} %param.7) | copy-start | bytes 1540
  0.9 27.1 %copy-start.3 = (s32[256]{0:T(256)S(1)}, s32[256]{0:T(256)}, u32[]{:S(2)}) copy-start(s32[256]{0:T(256)} %param.9) | copy-start | bytes 3076
  0.9 27.1 %copy-start.4 = (s32[256]{0:T(256)S(1)}, s32[256]{0:T(256)}, u32[]{:S(2)}) copy-start(s32[256]{0:T(256)} %param.8) | copy-start | bytes 3076
  2.3 25.7 %all-to-all-start = ((bf16[8,16,32,128]{3,2,1,0:T(8,128)(2,1)}), bf16[8,16,32,128]{3,2,1,0:T(8,128)(2,1)S(1)}, u32[]{:S(2)}, u32[]{:S(2)}) async-start(bf16[8,16,32,128]{3,2,1,0:T(8,128)(2,1)} %shard_map.64), calls=%async_computation | async-start | bytes 2097152 | tf_op jit(solution)/shard_map/all_to_all | solution.py:162
  29.0 39.2 %copy-start = (bf16[2048,1024]{1,0:T(8,128)(2,1)S(1)}, bf16[2048,1024]{1,0:T(8,128)(2,1)}, u32[]{:S(2)}) copy-start(bf16[2048,1024]{1,0:T(8,128)(2,1)} %constant.19.clone.weights) | copy-start | bytes 12582916
  72.4 6.6 %collective-permute-start = (bf16[128,1024]{1,0:T(8,128)(2,1)S(1)}, bf16[128,1024]{1,0:T(8,128)(2,1)S(1)}, u32[]{:S(2)}, u32[]{:S(2)}) collective-permute-start(bf16[128,1024]{1,0:T(8,128)(2,1)S(1)} %get-tuple-element.12), channel_id=1, source_target_pairs={{0,1},{1,0},{2,3},{3,2},{4,5},{5,4},{6,7},{7,6},{8,9},{9,8},{10,11... | collective-permute-start | bytes 786440 | tf_op jit(solution)/shard_map/ppermute | solution.py:187

commit v6 on v5

--- a/solution.py
+++ b/solution.py
@@ -82,8 +82,27 @@
     where[...] = jnp.where(first_core & is_slot, turned, slot)
 
 
-def stack_kernel(owned, pairs, slots, weights, mine, theirs, sums):
+def transform(owned, core, live, sums, weights):
+    half = sums.shape[0] // 2
+    starts = [pl.multiple_of(block * 2 * owned + core * owned, owned) for block in range(half // owned)]
+    q = lax.broadcasted_iota(jnp.int32, (half, LANES), 0)
+    is_live = (q // owned) * (2 * owned) + core * owned + q % owned < live
+
+    def folded(j):
+        rows = jnp.concatenate([sums[pl.ds(start, owned), j, :] for start in starts], axis=0)
+        return jnp.where(is_live, rows, 0.0).astype(jnp.bfloat16)
+
+    total = None
+    for j in range(0, 2 * BLOCKS, STEP):
+        block = jnp.concatenate([folded(j + i) for i in range(STEP)], axis=1)
+        part = jnp.dot(block, weights[j * LANES : (j + STEP) * LANES, :], preferred_element_type=jnp.float32)
+        total = part if total is None else total + part
+    return total * SCALE
+
+
+def stack_kernel(owned, pairs, slots, weights, theirs, sums):
     count, hours = sums.shape[0], slots.shape[1]
+    core = lax.axis_index("core")
     place = lax.broadcasted_iota(jnp.int32, (BLOCKS, LANES), 0) + lax.broadcasted_iota(jnp.int32, (BLOCKS, LANES), 1)
     corner = place == 0
 
@@ -102,22 +121,12 @@
         sums[p, :BLOCKS] = low + high
         sums[p, BLOCKS:] = jnp.where(corner, low - high, total_imag[:BLOCKS] - total_imag[BLOCKS:])
 
-    live = lax.broadcasted_iota(jnp.int32, (count, LANES), 0) < pairs[2 * count]
-    total = None
-    for j in range(0, 2 * BLOCKS, STEP):
-        folded = jnp.concatenate(
-            [jnp.where(live, sums[:, j + i, :], 0.0).astype(jnp.bfloat16) for i in range(STEP)], axis=1
-        )
-        part = jnp.dot(folded, weights[j * LANES : (j + STEP) * LANES, :], preferred_element_type=jnp.float32)
-        total = part if total is None else total + part
-    total = total * SCALE
-    core = lax.axis_index("core")
-    for block in range(count // (2 * owned)):
-        first = total[2 * block * owned : (2 * block + 1) * owned]
-        second = total[(2 * block + 1) * owned : (2 * block + 2) * owned]
-        rows = slice(block * owned, (block + 1) * owned)
-        mine[rows] = jnp.where(core == 0, first, second)
-        theirs[rows] = jnp.where(core == 0, second, first).astype(theirs.dtype)
+    theirs[...] = transform(owned, 1 - core, pairs[2 * count], sums, weights).astype(theirs.dtype)
+
+
+def own_kernel(owned, pairs, sums, weights, mine):
+    count = sums.shape[0]
+    mine[...] = transform(owned, lax.axis_index("core"), pairs[2 * count], sums, weights)
 
 
 def grid_groups(depth, height, width, cores):
@@ -176,15 +185,22 @@
     owned = pairs // windows
 
     half = (pairs // cores, LAGS)
-    ours, others = pl.pallas_call(
+    others, sums = pl.pallas_call(
         functools.partial(stack_kernel, owned),
-        out_shape=(jax.ShapeDtypeStruct(half, jnp.float32), jax.ShapeDtypeStruct(half, jnp.bfloat16)),
+        out_shape=(jax.ShapeDtypeStruct(half, jnp.bfloat16), jax.ShapeDtypeStruct((pairs, 2 * BLOCKS, LANES), jnp.float32)),
         in_specs=[smem, vmem, vmem],
         out_specs=(vmem, vmem),
-        scratch_shapes=[pltpu.VMEM((pairs, 2 * BLOCKS, LANES), jnp.float32)],
         compiler_params=params,
     )(where.reshape(-1), slots.reshape(tiles * cap, hours, ROWS, LANES), table)
     theirs = lax.ppermute(others, "core", [(0, 1), (1, 0)])
+    ours = pl.pallas_call(
+        functools.partial(own_kernel, owned),
+        out_shape=jax.ShapeDtypeStruct(half, jnp.float32),
+        in_specs=[smem, vmem, vmem],
+        out_specs=vmem,
+        compiler_params=params,
+        cost_estimate=pl.CostEstimate(flops=550000000, bytes_accessed=5000000, transcendentals=0),
+    )(where.reshape(-1), sums, table)
     both = (ours + theirs.astype(jnp.float32)).astype(jnp.bfloat16)
     parts = lax.all_to_all(both.reshape(width, owned, LAGS), "x", 0, 0, tiled=True)
     return jnp.sum(parts.astype(jnp.float32), axis=0)

time: 89.6 us -> 90 us (level)
  waiting for transfers between devices: 1.14 us -> 0.01 us
    pallas_call x0 -> x1, Pallas kernels: none -> 1.64 us  [body(): pl.pallas_call(functools.partial(own_kernel, owned), out_shape=jax.ShapeD...]
    ppermute x1, waiting for transfers between devices: 1.14 us -> 0.01 us  [body(): theirs = lax.ppermute(others, 'core', [(0, 1), (1, 0)])]
  transfers between devices with their start and end apart: 2 -> 2, of which waited for: 1 -> 0; matrix products, arithmetic and copies ran while one was open for 0% -> 0% of each run, Pallas kernels for 0% -> 2%
where the time goes in v6:
time: 90 us; the launch traced here: 89.7 us
  blocking collectives  66.8 us (74%)
  starting transfers between devices  13.1 us (15%)
  Pallas kernels  7.35 us (8%)
  local copies, waits for them, and re-layouts  0.92 us (1%)
    all_to_all x1, blocking collectives, body(): lax.all_to_all(send, AXES, 0, 0, axis_index_groups=stage_two, tiled=True)  39.2 us
    psum x1, blocking collectives, body(): wanted = lax.psum(own, AXES, axis_index_groups=stage_two)  17.3 us
    all_to_all x1, blocking collectives, body(): lax.all_to_all(both.reshape(width, owned, LAGS), 'x', 0, 0, tiled=True)  10.3 us
    all_to_all x1, starting transfers between devices, body(): lax.all_to_all(copies, AXES, 0, 0, axis_index_groups=stage_one, tiled=True)  7.65 us
    ppermute x1, starting transfers between devices, body(): theirs = lax.ppermute(others, 'core', [(0, 1), (1, 0)])  5.45 us
    pallas_call x1, Pallas kernels, body(): pl.pallas_call(functools.partial(stack_kernel, owned), out_shape=(jax.Sha...  3.38 us
  transfers between devices with their start and end apart: 2, of which 0 were waited for; matrix products, arithmetic and copies ran while one was open for 0% of the time, Pallas kernels for 2%

profile of v6, /device:TPU:1, one launch (start us, length us, event | category | flops | bytes accessed | tf_op | source)
XLA Modules:
  0.0 89.7 jit_solution(17751302987685719649)
XLA Ops:
  0.0 0.0 copy-start.1
  0.0 0.9 %copy-done.1 = bf16[2,8,4096]{2,1,0:T(8,128)(2,1)S(1)} copy-done((bf16[2,8,4096]{2,1,0:T(8,128)(2,1)S(1)}, bf16[2,8,4096]{2,1,0:T(8,128)(2,1)}, u32[]{:S(2)}) %copy-start.1) | copy-done | bytes 131096
  0.9 0.0 copy-start.2
  0.9 0.0 copy-start.3
  0.9 0.0 copy-start.4
  0.9 1.4 %shard_map.64 = bf16[8,16,32,128]{3,2,1,0:T(8,128)(2,1)} custom-call(bf16[2,8,4096]{2,1,0:T(8,128)(2,1)S(1)} %copy-done.1), custom_call_target="tpu_custom_call" | custom-call | tf_op jit(solution)/shard_map/pallas_call | solution.py:163
  2.3 7.7 %all-to-all-start = ((bf16[8,16,32,128]{3,2,1,0:T(8,128)(2,1)}), bf16[8,16,32,128]{3,2,1,0:T(8,128)(2,1)S(1)}, u32[]{:S(2)}, u32[]{:S(2)}) async-start(bf16[8,16,32,128]{3,2,1,0:T(8,128)(2,1)} %shard_map.64), calls=%async_computation | async-start | bytes 2097152 | tf_op jit(solution)/shard_map/all_to_all | solution.py:171
  10.7 0.0 copy-done.2
  10.7 0.1 broadcast_select_fusion
  10.7 17.3 %psum.7.wanted = s32[8,2,64]{2,1,0:T(2,128)S(1)} all-reduce(s32[8,2,64]{2,1,0:T(2,128)S(1)} %broadcast_select_fusion), channel_id=1, replica_groups={{0,8,16,24,32,40,48,56},{2,10,18,26,34,42,50,58},{4,12,20,28,36,44,52,6..., use_global_device_ids=true, to_apply=%region_0.1 | all-reduce | flops 1024 | bytes 8192 | tf_op jit(solution)/shard_map/psum | solution.py:162
  28.0 0.0 copy-done.3
  28.1 0.0 copy-done.4
  28.1 0.0 all-to-all-done.held
  28.1 0.9 shard_map.65
  29.0 0.0 copy-start
  29.0 39.2 %all_to_all.15 = bf16[8,8,2,2,32,128]{5,4,3,2,1,0:T(8,128)(2,1)S(1)} all-to-all(bf16[8,8,2,2,32,128]{5,4,3,2,1,0:T(8,128)(2,1)S(1)} %get-tuple-element.10), channel_id=1, replica_groups={{0,8,16,24,32,40,48,56},{2,10,18,26,34,42,50,58},{4,12,20,28,36,44,52,6..., dimensions={0} | all-to-all | bytes 4194304 | tf_op jit(solution)/shard_map/all_to_all | solution.py:184
  68.2 0.0 copy-done
  68.2 3.4 %shard_map.66 = (bf16[128,1024]{1,0:T(8,128)(2,1)S(1)}, f32[256,16,128]{2,1,0:T(8,128)S(1)}) custom-call(s32[1024]{0:T(1024)S(1)} %bitcast.11, bf16[128,2,32,128]{3,2,1,0:T(8,128)(2,1)S(1)} %bitcast.10, bf16[2048,1024]{1,0:T(8,128)(2,1)S(1)} %copy-done), custom_call_target="tpu_custom_call" | custom-call | tf_op jit(solution)/shard_map/pallas_call | solution.py:188
  71.5 5.4 %collective-permute-start = (bf16[128,1024]{1,0:T(8,128)(2,1)S(1)}, bf16[128,1024]{1,0:T(8,128)(2,1)S(1)}, u32[]{:S(2)}, u32[]{:S(2)}) collective-permute-start(bf16[128,1024]{1,0:T(8,128)(2,1)S(1)} %get-tuple-element.12), channel_id=1, source_target_pairs={{0,1},{1,0},{2,3},{3,2},{4,5},{5,4},{6,7},{7,6},{8,9},{9,8},{10,11... | collective-permute-start | bytes 786440 | tf_op jit(solution)/shard_map/ppermute | solution.py:195
  77.0 1.6 %shard_map.67 = f32[128,1024]{1,0:T(8,128)S(1)} custom-call(s32[1024]{0:T(1024)S(1)} %bitcast.12, f32[256,16,128]{2,1,0:T(8,128)S(1)} %get-tuple-element.11.sums, bf16[2048,1024]{1,0:T(8,128)(2,1)S(1)} %copy-done), custom_call_target="tpu_custom_call" | custom-call | flops 550000000 | bytes 5000000 | tf_op jit(solution)/shard_map/pallas_call | solution.py:196
  78.6 0.0 collective-permute-done
  78.7 0.1 add_convert_fusion
  78.7 10.3 %all_to_all.16 = bf16[4,32,1024]{2,1,0:T(8,128)(2,1)S(1)} all-to-all(bf16[4,32,1024]{2,1,0:T(8,128)(2,1)S(1)} %bitcast.13), channel_id=1, replica_groups=mesh['z'=8,'y'=8,'x'=4,'core'=2] {'x'}, dimensions={0} | all-to-all | bytes 524288 | tf_op jit(solution)/shard_map/all_to_all | solution.py:205
  89.0 0.7 convert_reduce_fusion
  (3 shorter events, 0.0 us)
Async XLA Ops:
  0.0 0.9 %copy-start.1 = (bf16[2,8,4096]{2,1,0:T(8,128)(2,1)S(1)}, bf16[2,8,4096]{2,1,0:T(8,128)(2,1)}, u32[]{:S(2)}) copy-start(bf16[2,8,4096]{2,1,0:T(8,128)(2,1)} %spectra.1) | copy-start | bytes 393220
  0.9 9.8 %copy-start.2 = (s32[1,64,2]{1,2,0:T(2,128)S(1)}, s32[1,64,2]{1,2,0:T(2,128)}, u32[]{:S(2)}) copy-start(s32[1,64,2]{1,2,0:T(2,128)} %param.7) | copy-start | bytes 1540
  0.9 27.1 %copy-start.3 = (s32[256]{0:T(256)S(1)}, s32[256]{0:T(256)}, u32[]{:S(2)}) copy-start(s32[256]{0:T(256)} %param.9) | copy-start | bytes 3076
  0.9 27.1 %copy-start.4 = (s32[256]{0:T(256)S(1)}, s32[256]{0:T(256)}, u32[]{:S(2)}) copy-start(s32[256]{0:T(256)} %param.8) | copy-start | bytes 3076
  2.3 25.7 %all-to-all-start = ((bf16[8,16,32,128]{3,2,1,0:T(8,128)(2,1)}), bf16[8,16,32,128]{3,2,1,0:T(8,128)(2,1)S(1)}, u32[]{:S(2)}, u32[]{:S(2)}) async-start(bf16[8,16,32,128]{3,2,1,0:T(8,128)(2,1)} %shard_map.64), calls=%async_computation | async-start | bytes 2097152 | tf_op jit(solution)/shard_map/all_to_all | solution.py:171
  29.0 39.2 %copy-start = (bf16[2048,1024]{1,0:T(8,128)(2,1)S(1)}, bf16[2048,1024]{1,0:T(8,128)(2,1)}, u32[]{:S(2)}) copy-start(bf16[2048,1024]{1,0:T(8,128)(2,1)} %constant.19.clone.weights) | copy-start | bytes 12582916
  71.5 7.1 %collective-permute-start = (bf16[128,1024]{1,0:T(8,128)(2,1)S(1)}, bf16[128,1024]{1,0:T(8,128)(2,1)S(1)}, u32[]{:S(2)}, u32[]{:S(2)}) collective-permute-start(bf16[128,1024]{1,0:T(8,128)(2,1)S(1)} %get-tuple-element.12), channel_id=1, source_target_pairs={{0,1},{1,0},{2,3},{3,2},{4,5},{5,4},{6,7},{7,6},{8,9},{9,8},{10,11... | collective-permute-start | bytes 786440 | tf_op jit(solution)/shard_map/ppermute | solution.py:195
